TPU v7x, 32 devices: a whole 2x2x4 slice. The times are simulated.
32 devices in a mesh: group: 2 (over x), row: 16 (over z, y, core).
Axes of the slice: x: 2, y: 2, z: 4, core: 2. Of those that a mesh axis runs over, the one named last changes fastest.
Arguments:
- orbitals: bfloat16 [8192, 2048], P(('group', 'row')), parts along dimension 0, may hold values from -6 to 6
- rotation: bfloat16 [8192, 2048], P(('group', 'row')), parts along dimension 0, may hold values from -6 to 6
- fock_tiles: bfloat16 [64, 5, 128, 128], P(('group', 'row')), parts along dimension 0, may hold values from -1 to 1, as said below
- fock_pattern: int32 [64, 5], P(('group', 'row')), parts along dimension 0, may hold values from 0 to 1, as said below
- correlation_tiles: bfloat16 [64, 5, 128, 128], P(('group', 'row')), parts along dimension 0, may hold values from -1 to 2, as said below
- correlation_pattern: int32 [64, 5], P(('group', 'row')), parts along dimension 0, may hold values from 0 to 1, as said below
Outputs:
- rotated: bfloat16 [8192, 2048], P(('group', 'row')), parts along dimension 0
- fock_rotated: float32 [8192, 2048], P(('group', 'row')), parts along dimension 0
There are 2 independent parts, one for each index of `group`. A program takes and returns all parts, laid end to end along the dimension named above; each array names one. Nothing has to cross between parts.
Inputs may be any that keep to these rules, and one draw needn't show every extreme that they name: `correlation_tiles`: symmetric: slot j of block row b is the transpose of slot 4 - j of block row b + j - 2 where both lie inside the matrix. `fock_tiles`: symmetric: slot j of block row b is the transpose of slot 4 - j of block row b + j - 2 where both lie inside the matrix. `fock_pattern`: slot j of block row b equals slot 4 - j of block row b + j - 2 where both lie inside the matrix. `correlation_pattern`: slot j of block row b equals slot 4 - j of block row b + j - 2 where both lie inside the matrix.
All inputs are finite; a program needn't handle non-finite values.
Results may differ from a plain program's by a relative error of at most 0.012.
The roundings to bfloat16 on the way count: a program that leaves them out, or rounds other values in their place, can miss the bound.
Values may be sent and summed in bfloat16 or wider, within the bound.
A program may use at most 128 MiB of HBM per device.

v0:
```python
import math

import jax
import jax.numpy as jnp
from jax import lax
from jax.sharding import PartitionSpec as P

ORDER = 5


def extended_2(value, sides, width):
    for axis, dim in sides:
        size, length = (lax.axis_size(axis), value.shape[dim])
        up = [(i, (i + 1) % size) for i in range(size - 1)]
        down = [(j, i) for i, j in up]
        last = lax.slice_in_dim(value, length - width, length, axis=dim)
        initial = lax.slice_in_dim(value, 0, width, axis=dim)
        before = lax.ppermute(last, axis, up)
        after = lax.ppermute(initial, axis, down)
        value = jnp.concatenate([before, value, after], axis=dim)
    return value


def near_product(tile_values, pattern, extended, blocks_dev, tile_size):
    orbital_count = extended.shape[1]
    blocks = extended.reshape(blocks_dev + 4, tile_size, orbital_count)
    slot_ids = lax.broadcasted_iota(jnp.int32, pattern.shape, 1)
    live_mask = (pattern > 0) | (slot_ids == 2)
    accumulated = jnp.zeros((blocks_dev, tile_size, orbital_count), jnp.float32)
    for slot_index in range(5):
        masked_tile = jnp.where(
            live_mask[:, slot_index, None, None],
            tile_values[:, slot_index],
            jnp.zeros((), jnp.bfloat16),
        )
        accumulated = accumulated + jnp.einsum(
            "bij,bjm->bim",
            masked_tile,
            blocks[slot_index : slot_index + blocks_dev],
            preferred_element_type=jnp.float32,
        )
    return accumulated.reshape(blocks_dev * tile_size, orbital_count)


def shards(orbitals, rotation, fock_tiles, fock_pattern, correlation_tiles, correlation_pattern):
    blocks_dev = correlation_tiles.shape[0]
    tile_size = correlation_tiles.shape[2]
    local_rows = rotation.shape[0]
    devices_row = lax.axis_size("row")
    basis_total = local_rows * devices_row
    cos_coeffs = [(-1.0) ** degree / math.factorial(2 * degree) for degree in range(ORDER + 1)]
    sin_coeffs = [(-1.0) ** degree / math.factorial(2 * degree + 1) for degree in range(ORDER + 1)]
    extended = extended_2(rotation, (("row", 0),), 2 * tile_size)
    correlation_applied = near_product(
        correlation_tiles, correlation_pattern, extended, blocks_dev, tile_size
    ).astype(jnp.bfloat16)
    partial_gram = jnp.dot(rotation.T, correlation_applied, preferred_element_type=jnp.float32)
    gram_share = lax.psum_scatter(partial_gram, "row", scatter_dimension=0, tiled=True)
    gram_low = (gram_share * (4.0 / basis_total)).astype(jnp.bfloat16)
    orbitals_wide = orbitals.astype(jnp.float32)
    rotation_wide = rotation.astype(jnp.float32)
    current = (cos_coeffs[ORDER] * orbitals_wide + sin_coeffs[ORDER] * rotation_wide).astype(
        jnp.bfloat16
    )
    gram_full = lax.all_gather(gram_low, "row", axis=0, tiled=True)
    first_sum = jnp.dot(current, gram_full, preferred_element_type=jnp.float32)
    current = (
        first_sum + cos_coeffs[ORDER - 1] * orbitals_wide + sin_coeffs[ORDER - 1] * rotation_wide
    ).astype(jnp.bfloat16)
    for degree in range(ORDER - 2, -1, -1):
        summed = jnp.dot(current, gram_full, preferred_element_type=jnp.float32)
        current = (
            summed + cos_coeffs[degree] * orbitals_wide + sin_coeffs[degree] * rotation_wide
        ).astype(jnp.bfloat16)
    rotated_ext = extended_2(current, (("row", 0),), 2 * tile_size)
    fock_rotated = near_product(fock_tiles, fock_pattern, rotated_ext, blocks_dev, tile_size)
    return (current, fock_rotated)


def solution(mesh):
    return jax.shard_map(
        shards,
        mesh=mesh,
        in_specs=(
            P(("group", "row"), None),
            P(("group", "row"), None),
            P(("group", "row"), None, None, None),
            P(("group", "row"), None),
            P(("group", "row"), None, None, None),
            P(("group", "row"), None),
        ),
        out_specs=(P(("group", "row"), None), P(("group", "row"), None)),
        check_vma=False,
    )
```

profile of v0, /device:TPU:25, one launch (start us, length us, event | category | flops | bytes accessed | tf_op | source)
XLA Modules:
  0.0 370.3 jit_solution(1261683084565672000)
XLA Ops:
  7.2 0.0 reduce-scatter.2.cloned.1.call-start
  7.2 3.8 %collective-permute-start = (bf16[256,2048]{1,0:T(8,128)(2,1)}, bf16[256,2048]{1,0:T(8,128)(2,1)S(1)}, u32[]{:S(2)}, u32[]{:S(2)}) collective-permute-start(bf16[256,2048]{1,0:T(8,128)(2,1)} %param.7), channel_id=1, source_target_pairs={{0,1},{1,2},{2,3},{3,4},{4,5},{5,6},{6,7},{7,8},{8,9},{9,10},{10,1... | collective-permute-start | bytes 3145736 | tf_op jit(solution)/shard_map/ppermute | solution.py:18
  11.1 1.9 collective-permute-start.1
  13.0 0.7 compare_or_fusion
  13.7 0.3 slice_reduce_fusion.6
  14.0 1.7 fusion.24
  15.7 7.4 %collective-permute-done = bf16[256,2048]{1,0:T(8,128)(2,1)S(1)} collective-permute-done((bf16[256,2048]{1,0:T(8,128)(2,1)}, bf16[256,2048]{1,0:T(8,128)(2,1)S(1)}, u32[]{:S(2)}, u32[]{:S(2)}) %collective-permute-start) | collective-permute-done | bytes 1048608 | tf_op jit(solution)/shard_map/ppermute | solution.py:18
  23.1 12.7 %collective-permute-done.1 = bf16[256,2048]{1,0:T(8,128)(2,1)S(1)} collective-permute-done((bf16[256,2048]{1,0:T(8,128)(2,1)}, bf16[256,2048]{1,0:T(8,128)(2,1)S(1)}, u32[]{:S(2)}, u32[]{:S(2)}) %collective-permute-start.1) | collective-permute-done | bytes 1048608 | tf_op jit(solution)/shard_map/ppermute | solution.py:19
  35.8 0.2 pad_maximum_fusion.2
  36.0 0.5 fusion.23
  36.5 0.5 fusion.22
  36.9 0.5 fusion.3
  37.5 0.6 fusion.8
  38.1 8.1 %convolution_bitcast_fusion = f32[2048,2048]{0,1:T(8,128)} fusion(bf16[256,2048]{1,0:T(8,128)(2,1)S(1)} %bitcast.83, bf16[256,2048]{1,0:T(8,128)(2,1)S(1)} %copy-done), kind=kOutput, calls=%fused_computation | convolution fusion | flops 2147483648 | bytes 18874368 | tf_op jit(solution)/shard_map/dot_general | solution.py:57
  46.2 0.2 all-gather.2.cloned.1.call-start
  46.4 176.3 %reduce-scatter.2.cloned.1.call-done = f32[128,2048]{0,1:T(8,128)} async-done(((f32[2048,2048]{0,1:T(8,128)}), f32[128,2048]{0,1:T(8,128)}) %reduce-scatter.2.cloned.1.call-update) | async-done | bytes 1048592 | tf_op jit(solution)/shard_map/reduce_scatter | solution.py:58
  222.8 2.1 multiply_convert_fusion
  224.9 77.9 %all-gather.2.cloned.1.call-done = bf16[2048,2048]{0,1:T(8,128)(2,1)} async-done(((bf16[128,2048]{0,1:T(8,128)(2,1)}), bf16[2048,2048]{0,1:T(8,128)(2,1)}) %all-gather.2.cloned.1.call-update) | async-done | bytes 8388624 | tf_op jit(solution)/shard_map/all_gather | solution.py:65
  302.8 6.0 %fusion.10 = bf16[256,2048]{1,0:T(8,128)(2,1)S(1)} fusion(bf16[2048,2048]{0,1:T(8,128)(2,1)} %all-gather.2.cloned.1.call-done, bf16[256,2048]{1,0:T(8,128)(2,1)S(1)} %copy-done.4, bf16[256,2048]{1,0:T(8,128)(2,1)S(1)} %copy-done), kind=kOutput, calls=%fused_computation.31 | convolution fusion | flops 2154299392 | bytes 11534336 | tf_op jit(solution)/shard_map/dot_general | solution.py:66
  308.8 12.0 %fusion.12 = bf16[256,2048]{1,0:T(8,128)(2,1)} fusion(bf16[2048,2048]{0,1:T(8,128)(2,1)} %all-gather.2.cloned.1.call-done, bf16[256,2048]{1,0:T(8,128)(2,1)S(1)} %copy-done.4, bf16[256,2048]{1,0:T(8,128)(2,1)S(1)} %copy-done, bf16[256,2048]{1,0:T(8,128)(2,1)S(1)} %fusion.10), kind=kOutput, calls=%fused_computation.33 | convolution fusion | flops 4302307328 | bytes 12582912 | tf_op jit(solution)/shard_map/dot_general | solution.py:71
  320.7 11.3 %fusion.9 = bf16[256,2048]{1,0:T(8,128)(2,1)S(1)} fusion(bf16[256,2048]{1,0:T(8,128)(2,1)S(1)} %copy-done, bf16[256,2048]{1,0:T(8,128)(2,1)S(1)} %copy-done.4, bf16[2048,2048]{0,1:T(8,128)(2,1)} %all-gather.2.cloned.1.call-done, bf16[256,2048]{1,0:T(8,128)(2,1)} %fusion.12), kind=kOutput, calls=%fused_computation.30 | convolution fusion | flops 4301258752 | bytes 12582912 | tf_op jit(solution)/shard_map/dot_general | solution.py:71
  332.0 2.7 collective-permute-start.2
  334.7 1.9 collective-permute-start.3
  336.6 0.3 slice_reduce_fusion.1
  336.9 0.5 fusion.20
  337.4 9.1 %collective-permute-done.2 = bf16[256,2048]{1,0:T(8,128)(2,1)S(1)} collective-permute-done((bf16[256,2048]{1,0:T(8,128)(2,1)S(1)}, bf16[256,2048]{1,0:T(8,128)(2,1)S(1)}, u32[]{:S(2)}, u32[]{:S(2)}) %collective-permute-start.2) | collective-permute-done | bytes 1048608 | tf_op jit(solution)/shard_map/ppermute | solution.py:18
  346.4 13.4 %collective-permute-done.3 = bf16[256,2048]{1,0:T(8,128)(2,1)S(1)} collective-permute-done((bf16[256,2048]{1,0:T(8,128)(2,1)S(1)}, bf16[256,2048]{1,0:T(8,128)(2,1)S(1)}, u32[]{:S(2)}, u32[]{:S(2)}) %collective-permute-start.3) | collective-permute-done | bytes 1048608 | tf_op jit(solution)/shard_map/ppermute | solution.py:19
  359.9 0.1 pad_maximum_fusion
  360.0 0.5 fusion.21
  360.5 0.5 fusion.19
  361.0 0.6 fusion.1
  361.5 1.9 fusion
  (13 shorter events, 0.1 us)
Async XLA Ops:
  7.2 28.6 %copy-start = (bf16[256,2048]{1,0:T(8,128)(2,1)S(1)}, bf16[256,2048]{1,0:T(8,128)(2,1)}, u32[]{:S(2)}) copy-start(bf16[256,2048]{1,0:T(8,128)(2,1)} %param.7) | copy-start | bytes 3145732
  7.2 215.6 %reduce-scatter.2.cloned.1.call-start = ((), (), s32[]{:S(2)}) async-start(), calls=%async_computation.1 | async-start | bytes 17825792 | tf_op jit(solution)/shard_map/reduce_scatter | solution.py:58
  7.2 15.9 %collective-permute-start = (bf16[256,2048]{1,0:T(8,128)(2,1)}, bf16[256,2048]{1,0:T(8,128)(2,1)S(1)}, u32[]{:S(2)}, u32[]{:S(2)}) collective-permute-start(bf16[256,2048]{1,0:T(8,128)(2,1)} %param.7), channel_id=1, source_target_pairs={{0,1},{1,2},{2,3},{3,4},{4,5},{5,6},{6,7},{7,8},{8,9},{9,10},{10,1... | collective-permute-start | bytes 3145736 | tf_op jit(solution)/shard_map/ppermute | solution.py:18
  11.1 24.7 %collective-permute-start.1 = (bf16[256,2048]{1,0:T(8,128)(2,1)}, bf16[256,2048]{1,0:T(8,128)(2,1)S(1)}, u32[]{:S(2)}, u32[]{:S(2)}) collective-permute-start(bf16[256,2048]{1,0:T(8,128)(2,1)} %param.7), channel_id=1, source_target_pairs={{1,0},{2,1},{3,2},{4,3},{5,4},{6,5},{7,6},{8,7},{9,8},{10,9},{11,1... | collective-permute-start | bytes 3145736 | tf_op jit(solution)/shard_map/ppermute | solution.py:19
  15.7 20.3 %copy-start.2 = (bf16[2,5,128,128]{3,2,1,0:T(8,128)(2,1)S(1)}, bf16[2,5,128,128]{3,2,1,0:T(8,128)(2,1)}, u32[]{:S(2)}) copy-start(bf16[2,5,128,128]{3,2,1,0:T(8,128)(2,1)} %param.10) | copy-start | bytes 983044
  46.2 256.6 %copy-start.4 = (bf16[256,2048]{1,0:T(8,128)(2,1)S(1)}, bf16[256,2048]{1,0:T(8,128)(2,1)}, u32[]{:S(2)}) copy-start(bf16[256,2048]{1,0:T(8,128)(2,1)} %param.6) | copy-start | bytes 3145732
  46.2 256.6 %all-gather.2.cloned.1.call-start = ((), (), s32[]{:S(2)}) async-start(), calls=%async_computation.2 | async-start | bytes 8912896 | tf_op jit(solution)/shard_map/all_gather | solution.py:65
  320.7 16.2 %copy-start.3 = (bf16[2,5,128,128]{3,2,1,0:T(8,128)(2,1)S(1)}, bf16[2,5,128,128]{3,2,1,0:T(8,128)(2,1)}, u32[]{:S(2)}) copy-start(bf16[2,5,128,128]{3,2,1,0:T(8,128)(2,1)} %param.8) | copy-start | bytes 983044
  332.0 28.0 %copy-start.1 = (bf16[256,2048]{1,0:T(8,128)(2,1)}, bf16[256,2048]{1,0:T(8,128)(2,1)S(1)}, u32[]{:S(2)}) copy-start(bf16[256,2048]{1,0:T(8,128)(2,1)S(1)} %fusion.9) | copy-start | bytes 3145732
  332.0 14.4 %collective-permute-start.2 = (bf16[256,2048]{1,0:T(8,128)(2,1)S(1)}, bf16[256,2048]{1,0:T(8,128)(2,1)S(1)}, u32[]{:S(2)}, u32[]{:S(2)}) collective-permute-start(bf16[256,2048]{1,0:T(8,128)(2,1)S(1)} %fusion.9), channel_id=1, source_target_pairs={{0,1},{1,2},{2,3},{3,4},{4,5},{5,6},{6,7},{7,8},{8,9},{9,10},{10,1... | collective-permute-start | bytes 3145736 | tf_op jit(solution)/shard_map/ppermute | solution.py:18
  334.7 25.1 %collective-permute-start.3 = (bf16[256,2048]{1,0:T(8,128)(2,1)S(1)}, bf16[256,2048]{1,0:T(8,128)(2,1)S(1)}, u32[]{:S(2)}, u32[]{:S(2)}) collective-permute-start(bf16[256,2048]{1,0:T(8,128)(2,1)S(1)} %fusion.9), channel_id=1, source_target_pairs={{1,0},{2,1},{3,2},{4,3},{5,4},{6,5},{7,6},{8,7},{9,8},{10,9},{11,1... | collective-permute-start | bytes 3145736 | tf_op jit(solution)/shard_map/ppermute | solution.py:19
Sparse Core Ops, SparseCore 0:
  46.3 176.3 reduce-scatter.1
  225.5 77.2 all-gather.1
where the time goes:
time: 372 us; the launch traced here: 370 us
  waiting for transfers between devices  297 us (80%)
  matrix products  45 us (12%)
  between operations  14.2 us (4%)
  starting transfers between devices  10.6 us (3%)
    reduce_scatter x1, waiting for transfers between devices, shards(): lax.psum_scatter(partial_gram, 'row', scatter_dimension=0, tiled=True)  176 us
    all_gather x1, waiting for transfers between devices, shards(): gram_full = lax.all_gather(gram_low, 'row', axis=0, tiled=True)  77.9 us
    ppermute x2, waiting for transfers between devices, extended_2(): after = lax.ppermute(initial, axis, down)  26.1 us
    dot_general x2, matrix products, shards(): summed = jnp.dot(current, gram_full, preferred_element_type=jnp.float32)  23.2 us
    ppermute x2, waiting for transfers between devices, extended_2(): before = lax.ppermute(last, axis, up)  16.4 us
    dot_general x1, matrix products, shards(): jnp.dot(rotation.T, correlation_applied, preferred_element_type=jnp.float32)  8.1 us
    dot_general x10, matrix products, near_product(): jnp.einsum('bij,bjm->bim', masked_tile, blocks[slot_index:slot_index + bl...  7.69 us
  transfers between devices with their start and end apart: 6, of which 6 were waited for; matrix products, arithmetic and copies ran while one was open for 1% of the time, Pallas kernels for 0%

commit v1 on v0

v1 whole, which is shorter than its diff:
```python
import functools
import math

import jax
import jax.numpy as jnp
from jax import lax
from jax.experimental import pallas as pl
from jax.experimental.pallas import tpu as pltpu
from jax.sharding import PartitionSpec as P

ORDER = 5
BLOCK = 128
SENT = jnp.bfloat16


def halo(value, width):
    size, length = lax.axis_size("row"), value.shape[0]
    up = [(i, i + 1) for i in range(size - 1)]
    down = [(j, i) for i, j in up]
    before = lax.ppermute(value[length - width :], "row", up)
    after = lax.ppermute(value[:width], "row", down)
    return jnp.concatenate([before, value, after], axis=0)


def near_product(tile_values, pattern, extended, blocks_dev, tile_size):
    orbital_count = extended.shape[1]
    blocks = extended.reshape(blocks_dev + 4, tile_size, orbital_count)
    slot_ids = lax.broadcasted_iota(jnp.int32, pattern.shape, 1)
    live_mask = (pattern > 0) | (slot_ids == 2)
    masked = jnp.where(live_mask[:, :, None, None], tile_values, jnp.zeros((), jnp.bfloat16))
    outs = []
    for b in range(blocks_dev):
        wide = jnp.swapaxes(masked[b], 0, 1).reshape(tile_size, 5 * tile_size)
        field = blocks[b : b + 5].reshape(5 * tile_size, orbital_count)
        outs.append(jnp.dot(wide, field, preferred_element_type=jnp.float32))
    return jnp.concatenate(outs, axis=0)


def gram_kernel(half, rot_ref, app_ref, out_ref):
    blocks = rot_ref.shape[1] // BLOCK
    width = (half + 1) * BLOCK
    for i in range(blocks):
        left = rot_ref[:, i * BLOCK : (i + 1) * BLOCK]
        start = i * BLOCK
        first = min(width, rot_ref.shape[1] - start)
        spans = [(0, start, first)]
        if first < width:
            spans.append((first, 0, width - first))
        for at, col, wide in spans:
            out_ref[i * BLOCK : (i + 1) * BLOCK, at : at + wide] = lax.dot_general(
                left,
                app_ref[:, col : col + wide],
                (((0,), (0,)), ((), ())),
                preferred_element_type=jnp.float32,
            ).astype(out_ref.dtype)


def horner_kernel(half, coeffs, packed_ref, orb_ref, rot_ref, out_ref, full):
    blocks = orb_ref.shape[1] // BLOCK
    cos_coeffs, sin_coeffs = coeffs
    for i in range(blocks):
        for k in range(half + 1):
            j = (i + k) % blocks
            tile = packed_ref[i * BLOCK : (i + 1) * BLOCK, k * BLOCK : (k + 1) * BLOCK]
            full[i * BLOCK : (i + 1) * BLOCK, j * BLOCK : (j + 1) * BLOCK] = tile
            if 0 < k < half:
                full[j * BLOCK : (j + 1) * BLOCK, i * BLOCK : (i + 1) * BLOCK] = tile.T
    orb = orb_ref[...].astype(jnp.float32)
    rot = rot_ref[...].astype(jnp.float32)
    current = (cos_coeffs[ORDER] * orb + sin_coeffs[ORDER] * rot).astype(jnp.bfloat16)
    columns = 512
    for degree in range(ORDER - 1, -1, -1):
        parts = []
        for c in range(0, orb_ref.shape[1], columns):
            total = jnp.dot(current, full[:, c : c + columns], preferred_element_type=jnp.float32)
            o = orb_ref[:, c : c + columns].astype(jnp.float32)
            r = rot_ref[:, c : c + columns].astype(jnp.float32)
            parts.append(
                (total + cos_coeffs[degree] * o + sin_coeffs[degree] * r).astype(jnp.bfloat16)
            )
        current = jnp.concatenate(parts, axis=1)
    out_ref[...] = current


def partners(size, bit):
    return [(i, i ^ bit) for i in range(size)]


def reduce_half(value, bit, sent):
    size = lax.axis_size("row")
    high = (lax.axis_index("row") & bit) != 0
    rows = value.shape[0] // 2
    low_part, high_part = value[:rows], value[rows:]
    send = jnp.where(high, low_part, high_part).astype(sent)
    keep = jnp.where(high, high_part, low_part)
    got = lax.ppermute(send, "row", partners(size, bit))
    return keep.astype(jnp.float32) + got.astype(jnp.float32)


def gather_half(value, bit):
    size = lax.axis_size("row")
    high = (lax.axis_index("row") & bit) != 0
    got = lax.ppermute(value, "row", partners(size, bit))
    return jnp.concatenate([jnp.where(high, got, value), jnp.where(high, value, got)], axis=0)


def shards(orbitals, rotation, fock_tiles, fock_pattern, correlation_tiles, correlation_pattern):
    blocks_dev = correlation_tiles.shape[0]
    tile_size = correlation_tiles.shape[2]
    local_rows, orbital_count = rotation.shape
    size = lax.axis_size("row")
    basis_total = local_rows * size
    half = orbital_count // BLOCK // 2
    width = (half + 1) * BLOCK
    cos_coeffs = [(-1.0) ** degree / math.factorial(2 * degree) for degree in range(ORDER + 1)]
    sin_coeffs = [(-1.0) ** degree / math.factorial(2 * degree + 1) for degree in range(ORDER + 1)]
    extended = halo(rotation, 2 * tile_size)
    applied = near_product(
        correlation_tiles, correlation_pattern, extended, blocks_dev, tile_size
    ).astype(jnp.bfloat16)
    packed = pl.pallas_call(
        functools.partial(gram_kernel, half),
        out_shape=jax.ShapeDtypeStruct((orbital_count, width), FIRST),
        in_specs=[pl.BlockSpec(memory_space=pltpu.VMEM)] * 2,
        out_specs=pl.BlockSpec(memory_space=pltpu.VMEM),
        compiler_params=pltpu.CompilerParams(vmem_limit_bytes=40 * 2**20),
    )(rotation, applied)

    share = reduce_half(packed, 1, FIRST)
    bits = [1 << b for b in range(1, size.bit_length() - 1)]
    other = [bits[1], bits[0]] + bits[2:] if len(bits) > 1 else bits
    rows = share.shape[0] // 2
    tracks = [(share[:rows], bits), (share[rows:], other)]
    values = [value for value, _ in tracks]
    for step in range(len(bits)):
        values = [
            reduce_half(value, order[step], SENT) for value, (_, order) in zip(values, tracks)
        ]
    values = [(value * (4.0 / basis_total)).astype(jnp.bfloat16) for value in values]
    for step in range(len(bits) - 1, -1, -1):
        values = [gather_half(value, order[step]) for value, (_, order) in zip(values, tracks)]
    gram_low = gather_half(jnp.concatenate(values, axis=0), 1)

    rotated = pl.pallas_call(
        functools.partial(horner_kernel, half, (cos_coeffs, sin_coeffs)),
        out_shape=jax.ShapeDtypeStruct((local_rows, orbital_count), jnp.bfloat16),
        in_specs=[pl.BlockSpec(memory_space=pltpu.VMEM)] * 3,
        out_specs=pl.BlockSpec(memory_space=pltpu.VMEM),
        scratch_shapes=[pltpu.VMEM((orbital_count, orbital_count), jnp.bfloat16)],
        compiler_params=pltpu.CompilerParams(vmem_limit_bytes=48 * 2**20),
    )(gram_low, orbitals, rotation)
    rotated_ext = halo(rotated, 2 * tile_size)
    fock_rotated = near_product(fock_tiles, fock_pattern, rotated_ext, blocks_dev, tile_size)
    return (rotated, fock_rotated)


FIRST = jnp.bfloat16


def solution(mesh):
    rows = P(("group", "row"), None)
    tiles = P(("group", "row"), None, None, None)
    return jax.shard_map(
        shards,
        mesh=mesh,
        in_specs=(rows, rows, tiles, rows, tiles, rows),
        out_specs=(rows, rows),
        check_vma=False,
    )
```

time: 372 us -> 183 us (0.49)
  waiting for transfers between devices: 297 us -> 113 us
  matrix products: 45 us -> 2.44 us
  other arithmetic: 3.09 us -> 20.5 us
  Pallas kernels: 0 us -> 17.1 us
  between operations: 14.2 us -> 1 us
  starting transfers between devices: 10.6 us -> 20.7 us
  local copies, waits for them, and re-layouts: 0.53 us -> 8 us
    reduce_scatter x1 -> x0, waiting for transfers between devices: 176 us -> none  [shards(): lax.psum_scatter(partial_gram, 'row', scatter_dimension=0, tiled=True)]
    all_gather x1 -> x0, waiting for transfers between devices: 77.9 us -> none  [shards(): gram_full = lax.all_gather(gram_low, 'row', axis=0, tiled=True)]
    ppermute x4 -> x18, waiting for transfers between devices: 42.6 us -> 113 us  [the longest x7 41 us: reduce_half(): got = lax.ppermute(send, 'row', partners(size, bit))]
    dot_general x14 -> x4, matrix products: 45 us -> 2.44 us  [near_product(): outs.append(jnp.dot(wide, field, preferred_element_type=jnp.float32))]
    pallas_call x0 -> x2, Pallas kernels: none -> 17.1 us  [the longest x1 15.5 us: shards(): pl.pallas_call(functools.partial(horner_kernel, half, (cos_coeffs, sin_co...]
    ppermute x4 -> x18, starting transfers between devices: 10.3 us -> 20.7 us  [the longest x7 6.62 us: reduce_half(): got = lax.ppermute(send, 'row', partners(size, bit))]
    unnamed x10 -> x14, local copies, waits for them, and re-layouts: 0.03 us -> 7.89 us
    select_n x0 -> x9, other arithmetic: none -> 6.8 us  [the longest x7 5.71 us: gather_half(): jnp.where(high, got, value)]
  transfers between devices with their start and end apart: 6 -> 18, of which waited for: 6 -> 16; matrix products, arithmetic and copies ran while one was open for 1% -> 4% of each run, Pallas kernels for 0% -> 0%
where the time goes in v1:
time: 183 us; the launch traced here: 182 us
  waiting for transfers between devices  113 us (62%)
  starting transfers between devices  20.7 us (11%)
  other arithmetic  20.5 us (11%)
  Pallas kernels  17.1 us (9%)
  local copies, waits for them, and re-layouts  8 us (4%)
  matrix products  2.44 us (1%)
    ppermute x7, waiting for transfers between devices, reduce_half(): got = lax.ppermute(send, 'row', partners(size, bit))  41 us
    ppermute x7, waiting for transfers between devices, gather_half(): got = lax.ppermute(value, 'row', partners(size, bit))  30.7 us
    ppermute x2, waiting for transfers between devices, halo(): after = lax.ppermute(value[:width], 'row', down)  25.2 us
    ppermute x2, waiting for transfers between devices, halo(): before = lax.ppermute(value[length - width:], 'row', up)  15.9 us
    pallas_call x1, Pallas kernels, shards(): pl.pallas_call(functools.partial(horner_kernel, half, (cos_coeffs, sin_co...  15.5 us
    unnamed x14, local copies, waits for them, and re-layouts  7.89 us
    add x4, other arithmetic, reduce_half(): return keep.astype(jnp.float32) + got.astype(jnp.float32)  6.63 us
    ppermute x7, starting transfers between devices, reduce_half(): got = lax.ppermute(send, 'row', partners(size, bit))  6.62 us
  transfers between devices with their start and end apart: 18, of which 16 were waited for; matrix products, arithmetic and copies ran while one was open for 4% of the time, Pallas kernels for 0%

profile of v1, /device:TPU:25, one launch (start us, length us, event | category | flops | bytes accessed | tf_op | source)
XLA Modules:
  0.0 182.4 jit_solution(17028350353973146365)
XLA Ops:
  0.6 3.7 %collective-permute-start = (bf16[256,2048]{1,0:T(8,128)(2,1)}, bf16[256,2048]{1,0:T(8,128)(2,1)}, u32[]{:S(2)}, u32[]{:S(2)}) collective-permute-start(bf16[256,2048]{1,0:T(8,128)(2,1)} %rot_ref.3), channel_id=1, source_target_pairs={{0,1},{1,2},{2,3},{3,4},{4,5},{5,6},{6,7},{7,8},{8,9},{9,10},{10,1... | collective-permute-start | bytes 3145736 | tf_op jit(solution)/shard_map/ppermute | solution.py:20
  4.3 1.9 %collective-permute-start.1 = (bf16[256,2048]{1,0:T(8,128)(2,1)}, bf16[256,2048]{1,0:T(8,128)(2,1)S(1)}, u32[]{:S(2)}, u32[]{:S(2)}) collective-permute-start(bf16[256,2048]{1,0:T(8,128)(2,1)} %rot_ref.3), channel_id=1, source_target_pairs={{1,0},{2,1},{3,2},{4,3},{5,4},{6,5},{7,6},{8,7},{9,8},{10,9},{11,1... | collective-permute-start | bytes 3145736 | tf_op jit(solution)/shard_map/ppermute | solution.py:21
  10.3 6.0 %collective-permute-done = bf16[256,2048]{1,0:T(8,128)(2,1)} collective-permute-done((bf16[256,2048]{1,0:T(8,128)(2,1)}, bf16[256,2048]{1,0:T(8,128)(2,1)}, u32[]{:S(2)}, u32[]{:S(2)}) %collective-permute-start) | collective-permute-done | bytes 1048608 | tf_op jit(solution)/shard_map/ppermute | solution.py:20
  16.4 1.3 constant_dynamic-update-slice_fusion.2
  17.8 11.2 %collective-permute-done.1 = bf16[256,2048]{1,0:T(8,128)(2,1)S(1)} collective-permute-done((bf16[256,2048]{1,0:T(8,128)(2,1)}, bf16[256,2048]{1,0:T(8,128)(2,1)S(1)}, u32[]{:S(2)}, u32[]{:S(2)}) %collective-permute-start.1) | collective-permute-done | bytes 1048608 | tf_op jit(solution)/shard_map/ppermute | solution.py:21
  30.5 1.6 shard_map.77
  32.4 1.9 %copy-done = bf16[2048,1152]{1,0:T(8,128)(2,1)} copy-done((bf16[2048,1152]{1,0:T(8,128)(2,1)}, bf16[2048,1152]{1,0:T(8,128)(2,1)S(1)}, u32[]{:S(2)}) %copy-start) | copy-done | bytes 4718616
  34.2 4.7 %collective-permute-done.2 = bf16[1024,1152]{1,0:T(8,128)(2,1)} collective-permute-done((bf16[1024,1152]{1,0:T(8,128)(2,1)S(1)}, bf16[1024,1152]{1,0:T(8,128)(2,1)}, u32[]{:S(2)}, u32[]{:S(2)}) %collective-permute-start.2) | collective-permute-done | bytes 2359328 | tf_op jit(solution)/shard_map/ppermute | solution.py:96
  38.9 3.9 %convert_add_fusion = f32[1024,1152]{1,0:T(8,128)S(1)} fusion(bf16[1024,1152]{1,0:T(8,128)(2,1)} %collective-permute-done.2, pred[]{:T(512)S(6)} %ne.8, bf16[2048,1152]{1,0:T(8,128)(2,1)} %copy-done), kind=kLoop, calls=%fused_computation.1 | loop fusion | flops 4718592 | bytes 11796481 | tf_op jit(solution)/shard_map/add | solution.py:97
  42.7 2.1 %copy-done.3 = f32[1024,1152]{1,0:T(8,128)} copy-done((f32[1024,1152]{1,0:T(8,128)}, f32[1024,1152]{1,0:T(8,128)S(1)}, u32[]{:S(2)}) %copy-start.3) | copy-done | bytes 4718616
  45.2 2.4 %collective-permute-start.9 = (bf16[256,1152]{1,0:T(8,128)(2,1)S(1)}, bf16[256,1152]{1,0:T(8,128)(2,1)S(1)}, u32[]{:S(2)}, u32[]{:S(2)}) collective-permute-start(bf16[256,1152]{1,0:T(8,128)(2,1)S(1)} %get-tuple-element.7), channel_id=1, source_target_pairs={{0,4},{1,5},{2,6},{3,7},{4,0},{5,1},{6,2},{7,3},{8,12},{9,13},{10,... | collective-permute-start | bytes 1769480 | tf_op jit(solution)/shard_map/ppermute | solution.py:96
  47.6 12.4 %collective-permute-done.3 = bf16[256,1152]{1,0:T(8,128)(2,1)S(1)} collective-permute-done((bf16[256,1152]{1,0:T(8,128)(2,1)S(1)}, bf16[256,1152]{1,0:T(8,128)(2,1)S(1)}, u32[]{:S(2)}, u32[]{:S(2)}) %collective-permute-start.3) | collective-permute-done | bytes 589856 | tf_op jit(solution)/shard_map/ppermute | solution.py:96
  60.6 2.6 %convert_add_fusion.2 = (f32[256,1152]{1,0:T(8,128)S(1)}, f32[256,1152]{1,0:T(8,128)S(1)}) fusion(bf16[256,1152]{1,0:T(8,128)(2,1)S(1)} %collective-permute-done.3, f32[1024,1152]{1,0:T(8,128)} %copy-done.3, pred[]{:T(512)S(6)} %ne.9, bf16[256,1152]{1,0:T(8,128)(2,1)S(1)} %collective-permute-done.9, pred[]{:T(512)S(6)} %ne.10), kind=kLoop, calls=%fused_computation.20 | loop fusion | flops 1769472 | bytes 8257538 | tf_op jit(solution)/shard_map/add | solution.py:97
  65.1 5.6 %collective-permute-done.4 = bf16[128,1152]{1,0:T(8,128)(2,1)S(1)} collective-permute-done((bf16[128,1152]{1,0:T(8,128)(2,1)S(1)}, bf16[128,1152]{1,0:T(8,128)(2,1)S(1)}, u32[]{:S(2)}, u32[]{:S(2)}) %collective-permute-start.4) | collective-permute-done | bytes 294944 | tf_op jit(solution)/shard_map/ppermute | solution.py:96
  71.7 1.7 collective-permute-start.11
  73.4 9.8 %collective-permute-done.5 = bf16[64,1152]{1,0:T(8,128)(2,1)S(1)} collective-permute-done((bf16[64,1152]{1,0:T(8,128)(2,1)S(1)}, bf16[64,1152]{1,0:T(8,128)(2,1)S(1)}, u32[]{:S(2)}, u32[]{:S(2)}) %collective-permute-start.5) | collective-permute-done | bytes 147488 | tf_op jit(solution)/shard_map/ppermute | solution.py:96
  83.4 7.8 %collective-permute-done.11 = bf16[64,1152]{1,0:T(8,128)(2,1)S(1)} collective-permute-done((bf16[64,1152]{1,0:T(8,128)(2,1)S(1)}, bf16[64,1152]{1,0:T(8,128)(2,1)S(1)}, u32[]{:S(2)}, u32[]{:S(2)}) %collective-permute-start.11) | collective-permute-done | bytes 147488 | tf_op jit(solution)/shard_map/ppermute | solution.py:96
  91.3 4.6 %collective-permute-done.6 = bf16[64,1152]{1,0:T(8,128)(2,1)S(1)} collective-permute-done((bf16[64,1152]{1,0:T(8,128)(2,1)S(1)}, bf16[64,1152]{1,0:T(8,128)(2,1)S(1)}, u32[]{:S(2)}, u32[]{:S(2)}) %collective-permute-start.6) | collective-permute-done | bytes 147488 | tf_op jit(solution)/shard_map/ppermute | solution.py:103
  96.1 3.0 %collective-permute-done.12 = bf16[64,1152]{1,0:T(8,128)(2,1)S(1)} collective-permute-done((bf16[64,1152]{1,0:T(8,128)(2,1)S(1)}, bf16[64,1152]{1,0:T(8,128)(2,1)S(1)}, u32[]{:S(2)}, u32[]{:S(2)}) %collective-permute-start.12) | collective-permute-done | bytes 147488 | tf_op jit(solution)/shard_map/ppermute | solution.py:103
  99.2 5.6 %collective-permute-done.7 = bf16[128,1152]{1,0:T(8,128)(2,1)S(1)} collective-permute-done((bf16[128,1152]{1,0:T(8,128)(2,1)S(1)}, bf16[128,1152]{1,0:T(8,128)(2,1)S(1)}, u32[]{:S(2)}, u32[]{:S(2)}) %collective-permute-start.7) | collective-permute-done | bytes 294944 | tf_op jit(solution)/shard_map/ppermute | solution.py:103
  106.7 12.4 %collective-permute-done.8 = bf16[256,1152]{1,0:T(8,128)(2,1)S(1)} collective-permute-done((bf16[256,1152]{1,0:T(8,128)(2,1)S(1)}, bf16[256,1152]{1,0:T(8,128)(2,1)S(1)}, u32[]{:S(2)}, u32[]{:S(2)}) %collective-permute-start.8) | collective-permute-done | bytes 589856 | tf_op jit(solution)/shard_map/ppermute | solution.py:103
  119.8 3.2 %collective-permute-start.15 = (bf16[1024,1152]{1,0:T(8,128)(2,1)S(1)}, bf16[1024,1152]{1,0:T(8,128)(2,1)S(1)}, u32[]{:S(2)}, u32[]{:S(2)}) collective-permute-start(bf16[1024,1152]{1,0:T(8,128)(2,1)S(1)} %pad_maximum_fusion.2), channel_id=1, source_target_pairs={{0,1},{1,0},{2,3},{3,2},{4,5},{5,4},{6,7},{7,6},{8,9},{9,8},{10,11... | collective-permute-start | bytes 7077896 | tf_op jit(solution)/shard_map/ppermute | solution.py:103
  122.9 4.2 %collective-permute-done.15 = bf16[1024,1152]{1,0:T(8,128)(2,1)S(1)} collective-permute-done((bf16[1024,1152]{1,0:T(8,128)(2,1)S(1)}, bf16[1024,1152]{1,0:T(8,128)(2,1)S(1)}, u32[]{:S(2)}, u32[]{:S(2)}) %collective-permute-start.15) | collective-permute-done | bytes 2359328 | tf_op jit(solution)/shard_map/ppermute | solution.py:103
  127.1 5.0 %broadcast_select_fusion.1 = (bf16[1024,1152]{1,0:T(8,128)(2,1)S(1)}, bf16[1024,1152]{1,0:T(8,128)(2,1)S(1)}) fusion(bf16[1024,1152]{1,0:T(8,128)(2,1)S(1)} %collective-permute-done.15, pred[]{:T(512)S(6)} %ne.8, bf16[256,1152]{1,0:T(8,128)(2,1)S(1)} %get-tuple-element.11, bf16[256,1152]{1,0:T(8,128)(2,1)S(1)} %get-tuple-element.10, ...), kind=kLoop, calls=%fused_computation.15 | loop fusion | flops 11796480 | bytes 9437185 | tf_op jit(solution)/shard_map/jit(_where)/select_n | solution.py:104
  132.1 2.5 %pad_maximum_fusion.packed_ref = bf16[2048,1152]{1,0:T(8,128)(2,1)} fusion(bf16[1024,1152]{1,0:T(8,128)(2,1)S(1)} %get-tuple-element.3, bf16[1024,1152]{1,0:T(8,128)(2,1)S(1)} %get-tuple-element.2), kind=kLoop, calls=%fused_computation | loop fusion | flops 9437184 | bytes 9437184 | tf_op jit(solution)/shard_map/concatenate | solution.py:104
  134.6 15.5 %shard_map.78 = bf16[256,2048]{1,0:T(8,128)(2,1)} custom-call(bf16[2048,1152]{1,0:T(8,128)(2,1)} %pad_maximum_fusion.packed_ref, bf16[256,2048]{1,0:T(8,128)(2,1)S(1)} %copy-done.2, bf16[256,2048]{1,0:T(8,128)(2,1)S(1)} %copy-done.1), custom_call_target="tpu_custom_call" | custom-call | tf_op jit(solution)/shard_map/pallas_call | solution.py:144
  150.1 2.1 %collective-permute-start.16 = (bf16[256,2048]{1,0:T(8,128)(2,1)}, bf16[256,2048]{1,0:T(8,128)(2,1)S(1)}, u32[]{:S(2)}, u32[]{:S(2)}) collective-permute-start(bf16[256,2048]{1,0:T(8,128)(2,1)} %shard_map.78), channel_id=1, source_target_pairs={{0,1},{1,2},{2,3},{3,4},{4,5},{5,6},{6,7},{7,8},{8,9},{9,10},{10,1... | collective-permute-start | bytes 3145736 | tf_op jit(solution)/shard_map/ppermute | solution.py:20
  152.3 2.2 %collective-permute-start.17 = (bf16[256,2048]{1,0:T(8,128)(2,1)}, bf16[256,2048]{1,0:T(8,128)(2,1)S(1)}, u32[]{:S(2)}, u32[]{:S(2)}) collective-permute-start(bf16[256,2048]{1,0:T(8,128)(2,1)} %shard_map.78), channel_id=1, source_target_pairs={{1,0},{2,1},{3,2},{4,3},{5,4},{6,5},{7,6},{8,7},{9,8},{10,9},{11,1... | collective-permute-start | bytes 3145736 | tf_op jit(solution)/shard_map/ppermute | solution.py:21
  154.5 9.8 %collective-permute-done.16 = bf16[256,2048]{1,0:T(8,128)(2,1)S(1)} collective-permute-done((bf16[256,2048]{1,0:T(8,128)(2,1)}, bf16[256,2048]{1,0:T(8,128)(2,1)S(1)}, u32[]{:S(2)}, u32[]{:S(2)}) %collective-permute-start.16) | collective-permute-done | bytes 1048608 | tf_op jit(solution)/shard_map/ppermute | solution.py:20
  164.3 14.0 %collective-permute-done.17 = bf16[256,2048]{1,0:T(8,128)(2,1)S(1)} collective-permute-done((bf16[256,2048]{1,0:T(8,128)(2,1)}, bf16[256,2048]{1,0:T(8,128)(2,1)S(1)}, u32[]{:S(2)}, u32[]{:S(2)}) %collective-permute-start.17) | collective-permute-done | bytes 1048608 | tf_op jit(solution)/shard_map/ppermute | solution.py:21
  178.3 1.4 pad_maximum_fusion.1
  180.9 1.5 pad_maximum_fusion.3
  (58 shorter events, 13.8 us)
Async XLA Ops:
  0.6 15.8 %collective-permute-start = (bf16[256,2048]{1,0:T(8,128)(2,1)}, bf16[256,2048]{1,0:T(8,128)(2,1)}, u32[]{:S(2)}, u32[]{:S(2)}) collective-permute-start(bf16[256,2048]{1,0:T(8,128)(2,1)} %rot_ref.3), channel_id=1, source_target_pairs={{0,1},{1,2},{2,3},{3,4},{4,5},{5,6},{6,7},{7,8},{8,9},{9,10},{10,1... | collective-permute-start | bytes 3145736 | tf_op jit(solution)/shard_map/ppermute | solution.py:20
  4.3 24.7 %collective-permute-start.1 = (bf16[256,2048]{1,0:T(8,128)(2,1)}, bf16[256,2048]{1,0:T(8,128)(2,1)S(1)}, u32[]{:S(2)}, u32[]{:S(2)}) collective-permute-start(bf16[256,2048]{1,0:T(8,128)(2,1)} %rot_ref.3), channel_id=1, source_target_pairs={{1,0},{2,1},{3,2},{4,3},{5,4},{6,5},{7,6},{8,7},{9,8},{10,9},{11,1... | collective-permute-start | bytes 3145736 | tf_op jit(solution)/shard_map/ppermute | solution.py:21
  8.2 9.5 %copy-start.1 = (bf16[256,2048]{1,0:T(8,128)(2,1)S(1)}, bf16[256,2048]{1,0:T(8,128)(2,1)}, u32[]{:S(2)}) copy-start(bf16[256,2048]{1,0:T(8,128)(2,1)} %rot_ref.3) | copy-start | bytes 3145732
  32.1 2.1 %copy-start = (bf16[2048,1152]{1,0:T(8,128)(2,1)}, bf16[2048,1152]{1,0:T(8,128)(2,1)S(1)}, u32[]{:S(2)}) copy-start(bf16[2048,1152]{1,0:T(8,128)(2,1)S(1)} %shard_map.77) | copy-start | bytes 14155780
  34.2 4.7 %collective-permute-start.2 = (bf16[1024,1152]{1,0:T(8,128)(2,1)S(1)}, bf16[1024,1152]{1,0:T(8,128)(2,1)}, u32[]{:S(2)}, u32[]{:S(2)}) collective-permute-start(bf16[1024,1152]{1,0:T(8,128)(2,1)S(1)} %broadcast_select_fusion.2), channel_id=1, source_target_pairs={{0,1},{1,0},{2,3},{3,2},{4,5},{5,4},{6,7},{7,6},{8,9},{9,8},{10,11... | collective-permute-start | bytes 7077896 | tf_op jit(solution)/shard_map/ppermute | solution.py:96
  42.7 2.1 %copy-start.3 = (f32[1024,1152]{1,0:T(8,128)}, f32[1024,1152]{1,0:T(8,128)S(1)}, u32[]{:S(2)}) copy-start(f32[1024,1152]{1,0:T(8,128)S(1)} %convert_add_fusion) | copy-start | bytes 14155780
  45.1 14.9 %collective-permute-start.3 = (bf16[256,1152]{1,0:T(8,128)(2,1)S(1)}, bf16[256,1152]{1,0:T(8,128)(2,1)S(1)}, u32[]{:S(2)}, u32[]{:S(2)}) collective-permute-start(bf16[256,1152]{1,0:T(8,128)(2,1)S(1)} %get-tuple-element.6), channel_id=1, source_target_pairs={{0,2},{1,3},{2,0},{3,1},{4,6},{5,7},{6,4},{7,5},{8,10},{9,11},{10,... | collective-permute-start | bytes 1769480 | tf_op jit(solution)/shard_map/ppermute | solution.py:96
  45.2 15.5 %collective-permute-start.9 = (bf16[256,1152]{1,0:T(8,128)(2,1)S(1)}, bf16[256,1152]{1,0:T(8,128)(2,1)S(1)}, u32[]{:S(2)}, u32[]{:S(2)}) collective-permute-start(bf16[256,1152]{1,0:T(8,128)(2,1)S(1)} %get-tuple-element.7), channel_id=1, source_target_pairs={{0,4},{1,5},{2,6},{3,7},{4,0},{5,1},{6,2},{7,3},{8,12},{9,13},{10,... | collective-permute-start | bytes 1769480 | tf_op jit(solution)/shard_map/ppermute | solution.py:96
  63.3 7.4 %collective-permute-start.4 = (bf16[128,1152]{1,0:T(8,128)(2,1)S(1)}, bf16[128,1152]{1,0:T(8,128)(2,1)S(1)}, u32[]{:S(2)}, u32[]{:S(2)}) collective-permute-start(bf16[128,1152]{1,0:T(8,128)(2,1)S(1)} %select_convert_fusion.3), channel_id=1, source_target_pairs={{0,4},{1,5},{2,6},{3,7},{4,0},{5,1},{6,2},{7,3},{8,12},{9,13},{10,... | collective-permute-start | bytes 884744 | tf_op jit(solution)/shard_map/ppermute | solution.py:96
  64.6 7.0 %collective-permute-start.10 = (bf16[128,1152]{1,0:T(8,128)(2,1)S(1)}, bf16[128,1152]{1,0:T(8,128)(2,1)S(1)}, u32[]{:S(2)}, u32[]{:S(2)}) collective-permute-start(bf16[128,1152]{1,0:T(8,128)(2,1)S(1)} %select_convert_fusion.2), channel_id=1, source_target_pairs={{0,2},{1,3},{2,0},{3,1},{4,6},{5,7},{6,4},{7,5},{8,10},{9,11},{10,... | collective-permute-start | bytes 884744 | tf_op jit(solution)/shard_map/ppermute | solution.py:96
  70.8 12.5 %collective-permute-start.5 = (bf16[64,1152]{1,0:T(8,128)(2,1)S(1)}, bf16[64,1152]{1,0:T(8,128)(2,1)S(1)}, u32[]{:S(2)}, u32[]{:S(2)}) collective-permute-start(bf16[64,1152]{1,0:T(8,128)(2,1)S(1)} %select_convert_fusion.5), channel_id=1, source_target_pairs={{0,8},{1,9},{2,10},{3,11},{4,12},{5,13},{6,14},{7,15},{8,0},{9,1},... | collective-permute-start | bytes 442376 | tf_op jit(solution)/shard_map/ppermute | solution.py:96
  71.7 19.5 %collective-permute-start.11 = (bf16[64,1152]{1,0:T(8,128)(2,1)S(1)}, bf16[64,1152]{1,0:T(8,128)(2,1)S(1)}, u32[]{:S(2)}, u32[]{:S(2)}) collective-permute-start(bf16[64,1152]{1,0:T(8,128)(2,1)S(1)} %select_convert_fusion.4), channel_id=1, source_target_pairs={{0,8},{1,9},{2,10},{3,11},{4,12},{5,13},{6,14},{7,15},{8,0},{9,1},... | collective-permute-start | bytes 442376 | tf_op jit(solution)/shard_map/ppermute | solution.py:96
  83.3 12.6 %collective-permute-start.6 = (bf16[64,1152]{1,0:T(8,128)(2,1)S(1)}, bf16[64,1152]{1,0:T(8,128)(2,1)S(1)}, u32[]{:S(2)}, u32[]{:S(2)}) collective-permute-start(bf16[64,1152]{1,0:T(8,128)(2,1)S(1)} %multiply_convert_fusion.1), channel_id=1, source_target_pairs={{0,8},{1,9},{2,10},{3,11},{4,12},{5,13},{6,14},{7,15},{8,0},{9,1},... | collective-permute-start | bytes 442376 | tf_op jit(solution)/shard_map/ppermute | solution.py:103
  91.2 7.8 %collective-permute-start.12 = (bf16[64,1152]{1,0:T(8,128)(2,1)S(1)}, bf16[64,1152]{1,0:T(8,128)(2,1)S(1)}, u32[]{:S(2)}, u32[]{:S(2)}) collective-permute-start(bf16[64,1152]{1,0:T(8,128)(2,1)S(1)} %multiply_convert_fusion), channel_id=1, source_target_pairs={{0,8},{1,9},{2,10},{3,11},{4,12},{5,13},{6,14},{7,15},{8,0},{9,1},... | collective-permute-start | bytes 442376 | tf_op jit(solution)/shard_map/ppermute | solution.py:103
  96.0 8.8 %collective-permute-start.7 = (bf16[128,1152]{1,0:T(8,128)(2,1)S(1)}, bf16[128,1152]{1,0:T(8,128)(2,1)S(1)}, u32[]{:S(2)}, u32[]{:S(2)}) collective-permute-start(bf16[128,1152]{1,0:T(8,128)(2,1)S(1)} %pad_maximum_fusion.7), channel_id=1, source_target_pairs={{0,4},{1,5},{2,6},{3,7},{4,0},{5,1},{6,2},{7,3},{8,12},{9,13},{10,... | collective-permute-start | bytes 884744 | tf_op jit(solution)/shard_map/ppermute | solution.py:103
  99.1 7.4 %collective-permute-start.13 = (bf16[128,1152]{1,0:T(8,128)(2,1)S(1)}, bf16[128,1152]{1,0:T(8,128)(2,1)S(1)}, u32[]{:S(2)}, u32[]{:S(2)}) collective-permute-start(bf16[128,1152]{1,0:T(8,128)(2,1)S(1)} %pad_maximum_fusion.8), channel_id=1, source_target_pairs={{0,2},{1,3},{2,0},{3,1},{4,6},{5,7},{6,4},{7,5},{8,10},{9,11},{10,... | collective-permute-start | bytes 884744 | tf_op jit(solution)/shard_map/ppermute | solution.py:103
  104.9 14.2 %collective-permute-start.8 = (bf16[256,1152]{1,0:T(8,128)(2,1)S(1)}, bf16[256,1152]{1,0:T(8,128)(2,1)S(1)}, u32[]{:S(2)}, u32[]{:S(2)}) collective-permute-start(bf16[256,1152]{1,0:T(8,128)(2,1)S(1)} %pad_maximum_fusion.5), channel_id=1, source_target_pairs={{0,2},{1,3},{2,0},{3,1},{4,6},{5,7},{6,4},{7,5},{8,10},{9,11},{10,... | collective-permute-start | bytes 1769480 | tf_op jit(solution)/shard_map/ppermute | solution.py:103
  106.7 12.7 %collective-permute-start.14 = (bf16[256,1152]{1,0:T(8,128)(2,1)S(1)}, bf16[256,1152]{1,0:T(8,128)(2,1)S(1)}, u32[]{:S(2)}, u32[]{:S(2)}) collective-permute-start(bf16[256,1152]{1,0:T(8,128)(2,1)S(1)} %pad_maximum_fusion.6), channel_id=1, source_target_pairs={{0,4},{1,5},{2,6},{3,7},{4,0},{5,1},{6,2},{7,3},{8,12},{9,13},{10,... | collective-permute-start | bytes 1769480 | tf_op jit(solution)/shard_map/ppermute | solution.py:103
  119.8 7.3 %collective-permute-start.15 = (bf16[1024,1152]{1,0:T(8,128)(2,1)S(1)}, bf16[1024,1152]{1,0:T(8,128)(2,1)S(1)}, u32[]{:S(2)}, u32[]{:S(2)}) collective-permute-start(bf16[1024,1152]{1,0:T(8,128)(2,1)S(1)} %pad_maximum_fusion.2), channel_id=1, source_target_pairs={{0,1},{1,0},{2,3},{3,2},{4,5},{5,4},{6,7},{7,6},{8,9},{9,8},{10,11... | collective-permute-start | bytes 7077896 | tf_op jit(solution)/shard_map/ppermute | solution.py:103
  132.1 2.5 %copy-start.2 = (bf16[256,2048]{1,0:T(8,128)(2,1)S(1)}, bf16[256,2048]{1,0:T(8,128)(2,1)}, u32[]{:S(2)}) copy-start(bf16[256,2048]{1,0:T(8,128)(2,1)} %orb_ref.1) | copy-start | bytes 3145732
  134.6 19.8 %copy-start.4 = (bf16[2,5,128,128]{2,3,1,0:T(8,128)(2,1)S(1)}, bf16[2,5,128,128]{2,3,1,0:T(8,128)(2,1)}, u32[]{:S(2)}) copy-start(bf16[2,5,128,128]{2,3,1,0:T(8,128)(2,1)} %get-tuple-element.26) | copy-start | bytes 983044
  150.1 14.2 %collective-permute-start.16 = (bf16[256,2048]{1,0:T(8,128)(2,1)}, bf16[256,2048]{1,0:T(8,128)(2,1)S(1)}, u32[]{:S(2)}, u32[]{:S(2)}) collective-permute-start(bf16[256,2048]{1,0:T(8,128)(2,1)} %shard_map.78), channel_id=1, source_target_pairs={{0,1},{1,2},{2,3},{3,4},{4,5},{5,6},{6,7},{7,8},{8,9},{9,10},{10,1... | collective-permute-start | bytes 3145736 | tf_op jit(solution)/shard_map/ppermute | solution.py:20
  152.3 26.0 %collective-permute-start.17 = (bf16[256,2048]{1,0:T(8,128)(2,1)}, bf16[256,2048]{1,0:T(8,128)(2,1)S(1)}, u32[]{:S(2)}, u32[]{:S(2)}) collective-permute-start(bf16[256,2048]{1,0:T(8,128)(2,1)} %shard_map.78), channel_id=1, source_target_pairs={{1,0},{2,1},{3,2},{4,3},{5,4},{6,5},{7,6},{8,7},{9,8},{10,9},{11,1... | collective-permute-start | bytes 3145736 | tf_op jit(solution)/shard_map/ppermute | solution.py:21

commit v2 on v1

--- a/solution.py
+++ b/solution.py
@@ -11,6 +11,7 @@
 ORDER = 5
 BLOCK = 128
 SENT = jnp.bfloat16
+TRACKS = 4
 
 
 def halo(value, width):
@@ -82,26 +83,134 @@
     out_ref[...] = current
 
 
-def partners(size, bit):
-    return [(i, i ^ bit) for i in range(size)]
-
-
-def reduce_half(value, bit, sent):
+def exchange_kernel(tracks, scale, packed_ref, out_ref, got, acc, send, send_sem, recv_sem):
     size = lax.axis_size("row")
-    high = (lax.axis_index("row") & bit) != 0
-    rows = value.shape[0] // 2
-    low_part, high_part = value[:rows], value[rows:]
-    send = jnp.where(high, low_part, high_part).astype(sent)
-    keep = jnp.where(high, high_part, low_part)
-    got = lax.ppermute(send, "row", partners(size, bit))
-    return keep.astype(jnp.float32) + got.astype(jnp.float32)
-
-
-def gather_half(value, bit):
+    me = lax.axis_index("row")
+    steps = size.bit_length() - 1
+    width = packed_ref.shape[1]
+    rows = packed_ref.shape[0] // tracks
+    half = rows // 2
+    outer = [1 << b for b in range(1, steps)]
+    swapped = [outer[1], outer[0]] + outer[2:] if len(outer) > 1 else outer
+    orders = [[1] + (outer if t % 2 == 0 else swapped) for t in range(tracks)]
+
+    def high(bit):
+        return lax.rem(me // bit, 2)
+
+    def partner(bit):
+        return me + bit - 2 * bit * high(bit)
+
+    def span(start, count):
+        return pl.ds(pl.multiple_of(start, 16), count)
+
+    def copy(source, target, t, step, bit):
+        return pltpu.make_async_remote_copy(
+            src_ref=source,
+            dst_ref=target,
+            send_sem=send_sem.at[t, step],
+            recv_sem=recv_sem.at[t, step],
+            device_id={"row": partner(bit)},
+            device_id_type=pl.DeviceIdType.MESH,
+        )
+
+    barrier = pltpu.get_barrier_semaphore()
+    for b in range(steps):
+        pl.semaphore_signal(
+            barrier, inc=1, device_id={"row": partner(1 << b)}, device_id_type=pl.DeviceIdType.MESH
+        )
+    pl.semaphore_wait(barrier, steps)
+
+    copies = []
+    pending = []
+    offsets = [0] * tracks
+    for t in range(tracks):
+        c = copy(
+            packed_ref.at[span(t * rows + (1 - high(1)) * half, half)],
+            got.at[pl.ds(t * rows, half)],
+            t, 0, 1,
+        )
+        c.start()
+        copies.append(c)
+        pending.append(c)
+
+    for step in range(steps):
+        count = rows >> (step + 1)
+        landed = rows - (rows >> step)
+        for t in range(tracks):
+            pending[t].wait_recv()
+            base = offsets[t]
+
+            def total(shift, number):
+                more = got[span(t * rows + landed + shift, number), :].astype(jnp.float32)
+                if step == 0:
+                    own = packed_ref[span(t * rows + high(1) * half + shift, number), :]
+                    return own.astype(jnp.float32) + more
+                return acc[span(t * half + base + shift, number), :] + more
+
+            if step < steps - 1:
+                bit = orders[t][step + 1]
+                part = count // 2
+                away, kept = (1 - high(bit)) * part, high(bit) * part
+                place = span(t * half + base + away, part)
+                send[place, :] = total(away, part).astype(send.dtype)
+                c = copy(
+                    send.at[place],
+                    got.at[pl.ds(t * rows + landed + count, part)],
+                    t, step + 1, bit,
+                )
+                c.start()
+                acc[span(t * half + base + kept, part), :] = total(kept, part)
+                offsets[t] = base + kept
+            else:
+                offsets[t] = t * rows + high(1) * half + base
+                place = span(offsets[t], count)
+                out_ref[place, :] = (total(0, count) * scale).astype(out_ref.dtype)
+                c = copy(out_ref.at[place], out_ref.at[place], t, steps, orders[t][step])
+                c.start()
+            copies.append(c)
+            pending[t] = c
+
+    count = rows >> steps
+    for step in range(steps):
+        for t in range(tracks):
+            bit = orders[t][steps - 1 - step]
+            pending[t].wait_recv()
+            offsets[t] = offsets[t] - high(bit) * count
+            if step < steps - 1:
+                place = span(offsets[t], 2 * count)
+                c = copy(
+                    out_ref.at[place], out_ref.at[place], t, steps + step + 1,
+                    orders[t][steps - 2 - step],
+                )
+                c.start()
+                copies.append(c)
+                pending[t] = c
+        count = 2 * count
+    for c in copies:
+        c.wait_send()
+
+
+def exchange(packed, scale):
     size = lax.axis_size("row")
-    high = (lax.axis_index("row") & bit) != 0
-    got = lax.ppermute(value, "row", partners(size, bit))
-    return jnp.concatenate([jnp.where(high, got, value), jnp.where(high, value, got)], axis=0)
+    rows, width = packed.shape
+    steps = size.bit_length() - 1
+    tracks = max(1, min(TRACKS, rows // (16 * size)))
+    return pl.pallas_call(
+        functools.partial(exchange_kernel, tracks, scale),
+        out_shape=jax.ShapeDtypeStruct((rows, width), jnp.bfloat16),
+        in_specs=[pl.BlockSpec(memory_space=pltpu.VMEM)],
+        out_specs=pl.BlockSpec(memory_space=pltpu.VMEM),
+        scratch_shapes=[
+            pltpu.VMEM((rows, width), SENT),
+            pltpu.VMEM((rows // 2, width), jnp.float32),
+            pltpu.VMEM((rows // 2, width), SENT),
+            pltpu.SemaphoreType.DMA((tracks, 2 * steps)),
+            pltpu.SemaphoreType.DMA((tracks, 2 * steps)),
+        ],
+        compiler_params=pltpu.CompilerParams(
+            collective_id=0, has_side_effects=True, vmem_limit_bytes=48 * 2**20
+        ),
+    )(packed)
 
 
 def shards(orbitals, rotation, fock_tiles, fock_pattern, correlation_tiles, correlation_pattern):
@@ -120,26 +229,13 @@
     ).astype(jnp.bfloat16)
     packed = pl.pallas_call(
         functools.partial(gram_kernel, half),
-        out_shape=jax.ShapeDtypeStruct((orbital_count, width), FIRST),
+        out_shape=jax.ShapeDtypeStruct((orbital_count, width), SENT),
         in_specs=[pl.BlockSpec(memory_space=pltpu.VMEM)] * 2,
         out_specs=pl.BlockSpec(memory_space=pltpu.VMEM),
         compiler_params=pltpu.CompilerParams(vmem_limit_bytes=40 * 2**20),
     )(rotation, applied)
 
-    share = reduce_half(packed, 1, FIRST)
-    bits = [1 << b for b in range(1, size.bit_length() - 1)]
-    other = [bits[1], bits[0]] + bits[2:] if len(bits) > 1 else bits
-    rows = share.shape[0] // 2
-    tracks = [(share[:rows], bits), (share[rows:], other)]
-    values = [value for value, _ in tracks]
-    for step in range(len(bits)):
-        values = [
-            reduce_half(value, order[step], SENT) for value, (_, order) in zip(values, tracks)
-        ]
-    values = [(value * (4.0 / basis_total)).astype(jnp.bfloat16) for value in values]
-    for step in range(len(bits) - 1, -1, -1):
-        values = [gather_half(value, order[step]) for value, (_, order) in zip(values, tracks)]
-    gram_low = gather_half(jnp.concatenate(values, axis=0), 1)
+    gram_low = exchange(packed, 4.0 / basis_total)
 
     rotated = pl.pallas_call(
         functools.partial(horner_kernel, half, (cos_coeffs, sin_coeffs)),
@@ -154,9 +250,6 @@
     return (rotated, fock_rotated)
 
 
-FIRST = jnp.bfloat16
-
-
 def solution(mesh):
     rows = P(("group", "row"), None)
     tiles = P(("group", "row"), None, None, None)

time: 183 us -> 158 us (0.86); the launches traced: 182 us -> 155 us
  waiting for transfers between devices: 113 us -> 40.1 us
  Pallas kernels: 17.1 us -> 88.3 us
  other arithmetic: 20.5 us -> 3.84 us
  starting transfers between devices: 20.7 us -> 11.6 us
    ppermute x14 -> x0, waiting for transfers between devices: 71.7 us -> none  [the longest x7 41 us: reduce_half(): got = lax.ppermute(send, 'row', partners(size, bit))]
    pallas_call x0 -> x1, Pallas kernels: none -> 71.1 us  [exchange(): pl.pallas_call(functools.partial(exchange_kernel, tracks, scale), out_sha...]
    ppermute x14 -> x0, starting transfers between devices: 10.7 us -> none  [the longest x7 6.62 us: reduce_half(): got = lax.ppermute(send, 'row', partners(size, bit))]
    ppermute x2, waiting for transfers between devices: 15.9 us -> 6.85 us  [halo(): before = lax.ppermute(value[length - width:], 'row', up)]
    ppermute x2, waiting for transfers between devices: 25.2 us -> 33.2 us  [halo(): after = lax.ppermute(value[:width], 'row', down)]
    add x4 -> x0, other arithmetic: 6.63 us -> none  [reduce_half(): return keep.astype(jnp.float32) + got.astype(jnp.float32)]
    select_n x8 -> x0, other arithmetic: 5.97 us -> none  [the longest x7 5.71 us: gather_half(): jnp.where(high, got, value)]
    concatenate x6 -> x0, other arithmetic: 2.82 us -> none  [the longest x5 2.64 us: gather_half(): jnp.concatenate([jnp.where(high, got, value), jnp.where(high, value, got)...]
  transfers between devices with their start and end apart: 18 -> 4, of which waited for: 16 -> 3; matrix products, arithmetic and copies ran while one was open for 4% -> 3% of each run, Pallas kernels for 0% -> 0%
where the time goes in v2:
time: 158 us; the launch traced here: 155 us
  Pallas kernels  88.3 us (56%)
  waiting for transfers between devices  40.1 us (25%)
  starting transfers between devices  11.6 us (7%)
  local copies, waits for them, and re-layouts  8.16 us (5%)
  other arithmetic  3.84 us (2%)
  matrix products  2.42 us (2%)
    pallas_call x1, Pallas kernels, exchange(): pl.pallas_call(functools.partial(exchange_kernel, tracks, scale), out_sha...  71.1 us
    ppermute x2, waiting for transfers between devices, halo(): after = lax.ppermute(value[:width], 'row', down)  33.2 us
    pallas_call x1, Pallas kernels, shards(): pl.pallas_call(functools.partial(horner_kernel, half, (cos_coeffs, sin_co...  15.7 us
    unnamed x12, local copies, waits for them, and re-layouts  8.04 us
    ppermute x2, starting transfers between devices, halo(): before = lax.ppermute(value[length - width:], 'row', up)  7.53 us
    ppermute x2, waiting for transfers between devices, halo(): before = lax.ppermute(value[length - width:], 'row', up)  6.85 us
    ppermute x2, starting transfers between devices, halo(): after = lax.ppermute(value[:width], 'row', down)  4.12 us
  transfers between devices with their start and end apart: 4, of which 3 were waited for; matrix products, arithmetic and copies ran while one was open for 3% of the time, Pallas kernels for 0%

profile of v2, /device:TPU:25, one launch (start us, length us, event | category | flops | bytes accessed | tf_op | source)
XLA Modules:
  0.0 155.3 jit_solution(12273168363115912576)
XLA Ops:
  0.6 0.0 copy-start.2
  0.6 3.8 %collective-permute-start = (bf16[256,2048]{1,0:T(8,128)(2,1)}, bf16[256,2048]{1,0:T(8,128)(2,1)}, u32[]{:S(2)}, u32[]{:S(2)}) collective-permute-start(bf16[256,2048]{1,0:T(8,128)(2,1)} %rot_ref.3), channel_id=1, source_target_pairs={{0,1},{1,2},{2,3},{3,4},{4,5},{5,6},{6,7},{7,8},{8,9},{9,10},{10,1... | collective-permute-start | bytes 3145736 | tf_op jit(solution)/shard_map/ppermute | solution.py:21
  4.5 1.9 %collective-permute-start.1 = (bf16[256,2048]{1,0:T(8,128)(2,1)}, bf16[256,2048]{1,0:T(8,128)(2,1)S(1)}, u32[]{:S(2)}, u32[]{:S(2)}) collective-permute-start(bf16[256,2048]{1,0:T(8,128)(2,1)} %rot_ref.3), channel_id=1, source_target_pairs={{1,0},{2,1},{3,2},{4,3},{5,4},{6,5},{7,6},{8,7},{9,8},{10,9},{11,1... | collective-permute-start | bytes 3145736 | tf_op jit(solution)/shard_map/ppermute | solution.py:22
  6.4 0.7 compare_or_fusion
  7.1 1.2 copy.9
  8.3 1.2 copy.8
  9.5 0.1 broadcast_select_fusion
  9.7 6.8 %collective-permute-done = bf16[256,2048]{1,0:T(8,128)(2,1)} collective-permute-done((bf16[256,2048]{1,0:T(8,128)(2,1)}, bf16[256,2048]{1,0:T(8,128)(2,1)}, u32[]{:S(2)}, u32[]{:S(2)}) %collective-permute-start) | collective-permute-done | bytes 1048608 | tf_op jit(solution)/shard_map/ppermute | solution.py:21
  16.5 1.3 constant_dynamic-update-slice_fusion.2
  17.9 0.0 copy-done.2
  17.9 0.1 constant_dynamic-update-slice_fusion.1
  17.9 11.3 %collective-permute-done.1 = bf16[256,2048]{1,0:T(8,128)(2,1)S(1)} collective-permute-done((bf16[256,2048]{1,0:T(8,128)(2,1)}, bf16[256,2048]{1,0:T(8,128)(2,1)S(1)}, u32[]{:S(2)}, u32[]{:S(2)}) %collective-permute-start.1) | collective-permute-done | bytes 1048608 | tf_op jit(solution)/shard_map/ppermute | solution.py:22
  29.2 0.1 constant_dynamic-update-slice_fusion
  29.3 0.6 fusion.11
  29.9 0.6 fusion.8
  30.5 0.1 pad_maximum_fusion.2.app_ref
  30.6 1.6 %shard_map.77.packed_ref = bf16[2048,1152]{1,0:T(8,128)(2,1)S(1)} custom-call(bf16[256,2048]{1,0:T(8,128)(2,1)S(1)} %copy-done.2, bf16[256,2048]{1,0:T(8,128)(2,1)S(1)} %pad_maximum_fusion.2.app_ref), custom_call_target="tpu_custom_call" | custom-call | tf_op jit(solution)/shard_map/pallas_call | solution.py:230
  32.2 0.0 copy-start
  32.2 2.1 %copy-done = bf16[2048,1152]{1,0:T(8,128)(2,1)} copy-done((bf16[2048,1152]{1,0:T(8,128)(2,1)}, bf16[2048,1152]{1,0:T(8,128)(2,1)S(1)}, u32[]{:S(2)}) %copy-start) | copy-done | bytes 4718616
  34.3 71.1 %shard_map.78.packed_ref = bf16[2048,1152]{1,0:T(8,128)(2,1)S(1)} custom-call(bf16[2048,1152]{1,0:T(8,128)(2,1)} %copy-done), custom_call_target="tpu_custom_call" | custom-call | tf_op jit(solution)/shard_map/pallas_call | solution.py:198
  105.4 0.0 copy-start.1
  105.4 2.1 %copy-done.1 = bf16[2048,1152]{1,0:T(8,128)(2,1)} copy-done((bf16[2048,1152]{1,0:T(8,128)(2,1)}, bf16[2048,1152]{1,0:T(8,128)(2,1)S(1)}, u32[]{:S(2)}) %copy-start.1) | copy-done | bytes 4718616
  107.6 0.0 copy-done.3
  107.6 15.7 %shard_map.79 = bf16[256,2048]{1,0:T(8,128)(2,1)} custom-call(bf16[2048,1152]{1,0:T(8,128)(2,1)} %copy-done.1, bf16[256,2048]{1,0:T(8,128)(2,1)S(1)} %copy-done.3, bf16[256,2048]{1,0:T(8,128)(2,1)S(1)} %copy-done.2), custom_call_target="tpu_custom_call" | custom-call | tf_op jit(solution)/shard_map/pallas_call | solution.py:240
  123.2 2.2 %collective-permute-start.3 = (bf16[256,2048]{1,0:T(8,128)(2,1)}, bf16[256,2048]{1,0:T(8,128)(2,1)S(1)}, u32[]{:S(2)}, u32[]{:S(2)}) collective-permute-start(bf16[256,2048]{1,0:T(8,128)(2,1)} %shard_map.79), channel_id=1, source_target_pairs={{1,0},{2,1},{3,2},{4,3},{5,4},{6,5},{7,6},{8,7},{9,8},{10,9},{11,1... | collective-permute-start | bytes 3145736 | tf_op jit(solution)/shard_map/ppermute | solution.py:22
  125.4 3.7 %collective-permute-start.2 = (bf16[256,2048]{1,0:T(8,128)(2,1)}, bf16[256,2048]{1,0:T(8,128)(2,1)S(1)}, u32[]{:S(2)}, u32[]{:S(2)}) collective-permute-start(bf16[256,2048]{1,0:T(8,128)(2,1)} %shard_map.79), channel_id=1, source_target_pairs={{0,1},{1,2},{2,3},{3,4},{4,5},{5,6},{6,7},{7,8},{8,9},{9,10},{10,1... | collective-permute-start | bytes 3145736 | tf_op jit(solution)/shard_map/ppermute | solution.py:21
  129.2 22.0 %collective-permute-done.3 = bf16[256,2048]{1,0:T(8,128)(2,1)S(1)} collective-permute-done((bf16[256,2048]{1,0:T(8,128)(2,1)}, bf16[256,2048]{1,0:T(8,128)(2,1)S(1)}, u32[]{:S(2)}, u32[]{:S(2)}) %collective-permute-start.3) | collective-permute-done | bytes 1048608 | tf_op jit(solution)/shard_map/ppermute | solution.py:22
  151.1 0.0 collective-permute-done.2
  151.1 1.4 pad_maximum_fusion
  152.6 0.6 fusion
  153.2 0.6 fusion.2
  153.8 1.5 pad_maximum_fusion.1
  (4 shorter events, 0.1 us)
Async XLA Ops:
  0.6 17.2 %copy-start.2 = (bf16[256,2048]{1,0:T(8,128)(2,1)S(1)}, bf16[256,2048]{1,0:T(8,128)(2,1)}, u32[]{:S(2)}) copy-start(bf16[256,2048]{1,0:T(8,128)(2,1)} %rot_ref.3) | copy-start | bytes 3145732
  0.6 15.9 %collective-permute-start = (bf16[256,2048]{1,0:T(8,128)(2,1)}, bf16[256,2048]{1,0:T(8,128)(2,1)}, u32[]{:S(2)}, u32[]{:S(2)}) collective-permute-start(bf16[256,2048]{1,0:T(8,128)(2,1)} %rot_ref.3), channel_id=1, source_target_pairs={{0,1},{1,2},{2,3},{3,4},{4,5},{5,6},{6,7},{7,8},{8,9},{9,10},{10,1... | collective-permute-start | bytes 3145736 | tf_op jit(solution)/shard_map/ppermute | solution.py:21
  4.5 24.7 %collective-permute-start.1 = (bf16[256,2048]{1,0:T(8,128)(2,1)}, bf16[256,2048]{1,0:T(8,128)(2,1)S(1)}, u32[]{:S(2)}, u32[]{:S(2)}) collective-permute-start(bf16[256,2048]{1,0:T(8,128)(2,1)} %rot_ref.3), channel_id=1, source_target_pairs={{1,0},{2,1},{3,2},{4,3},{5,4},{6,5},{7,6},{8,7},{9,8},{10,9},{11,1... | collective-permute-start | bytes 3145736 | tf_op jit(solution)/shard_map/ppermute | solution.py:22
  32.2 2.1 %copy-start = (bf16[2048,1152]{1,0:T(8,128)(2,1)}, bf16[2048,1152]{1,0:T(8,128)(2,1)S(1)}, u32[]{:S(2)}) copy-start(bf16[2048,1152]{1,0:T(8,128)(2,1)S(1)} %shard_map.77.packed_ref) | copy-start | bytes 14155780
  34.3 73.2 %copy-start.3 = (bf16[256,2048]{1,0:T(8,128)(2,1)S(1)}, bf16[256,2048]{1,0:T(8,128)(2,1)}, u32[]{:S(2)}) copy-start(bf16[256,2048]{1,0:T(8,128)(2,1)} %orb_ref.1) | copy-start | bytes 3145732
  105.4 2.1 %copy-start.1 = (bf16[2048,1152]{1,0:T(8,128)(2,1)}, bf16[2048,1152]{1,0:T(8,128)(2,1)S(1)}, u32[]{:S(2)}) copy-start(bf16[2048,1152]{1,0:T(8,128)(2,1)S(1)} %shard_map.78.packed_ref) | copy-start | bytes 14155780
  123.2 27.9 %collective-permute-start.3 = (bf16[256,2048]{1,0:T(8,128)(2,1)}, bf16[256,2048]{1,0:T(8,128)(2,1)S(1)}, u32[]{:S(2)}, u32[]{:S(2)}) collective-permute-start(bf16[256,2048]{1,0:T(8,128)(2,1)} %shard_map.79), channel_id=1, source_target_pairs={{1,0},{2,1},{3,2},{4,3},{5,4},{6,5},{7,6},{8,7},{9,8},{10,9},{11,1... | collective-permute-start | bytes 3145736 | tf_op jit(solution)/shard_map/ppermute | solution.py:22
  125.4 25.7 %collective-permute-start.2 = (bf16[256,2048]{1,0:T(8,128)(2,1)}, bf16[256,2048]{1,0:T(8,128)(2,1)S(1)}, u32[]{:S(2)}, u32[]{:S(2)}) collective-permute-start(bf16[256,2048]{1,0:T(8,128)(2,1)} %shard_map.79), channel_id=1, source_target_pairs={{0,1},{1,2},{2,3},{3,4},{4,5},{5,6},{6,7},{7,8},{8,9},{9,10},{10,1... | collective-permute-start | bytes 3145736 | tf_op jit(solution)/shard_map/ppermute | solution.py:21

commit v3 on v2

--- a/solution.py
+++ b/solution.py
@@ -11,7 +11,7 @@
 ORDER = 5
 BLOCK = 128
 SENT = jnp.bfloat16
-TRACKS = 4
+TRACKS = 8
 
 
 def halo(value, width):
@@ -56,16 +56,20 @@
             ).astype(out_ref.dtype)
 
 
-def horner_kernel(half, coeffs, packed_ref, orb_ref, rot_ref, out_ref, full):
-    blocks = orb_ref.shape[1] // BLOCK
-    cos_coeffs, sin_coeffs = coeffs
-    for i in range(blocks):
+def spread(packed_ref, full, first, last):
+    blocks = full.shape[0] // BLOCK
+    half = packed_ref.shape[1] // BLOCK - 1
+    for i in range(first, last):
         for k in range(half + 1):
             j = (i + k) % blocks
             tile = packed_ref[i * BLOCK : (i + 1) * BLOCK, k * BLOCK : (k + 1) * BLOCK]
             full[i * BLOCK : (i + 1) * BLOCK, j * BLOCK : (j + 1) * BLOCK] = tile
             if 0 < k < half:
                 full[j * BLOCK : (j + 1) * BLOCK, i * BLOCK : (i + 1) * BLOCK] = tile.T
+
+
+def horner(coeffs, orb_ref, rot_ref, out_ref, full):
+    cos_coeffs, sin_coeffs = coeffs
     orb = orb_ref[...].astype(jnp.float32)
     rot = rot_ref[...].astype(jnp.float32)
     current = (cos_coeffs[ORDER] * orb + sin_coeffs[ORDER] * rot).astype(jnp.bfloat16)
@@ -83,7 +87,10 @@
     out_ref[...] = current
 
 
-def exchange_kernel(tracks, scale, packed_ref, out_ref, got, acc, send, send_sem, recv_sem):
+def exchange_kernel(
+    tracks, scale, coeffs, packed_ref, orb_ref, rot_ref, rotated_ref,
+    got, acc, send, out_ref, full, send_sem, recv_sem,
+):
     size = lax.axis_size("row")
     me = lax.axis_index("row")
     steps = size.bit_length() - 1
@@ -185,32 +192,37 @@
                 c.start()
                 copies.append(c)
                 pending[t] = c
+            else:
+                spread(out_ref, full, t * rows // BLOCK, (t + 1) * rows // BLOCK)
         count = 2 * count
+    horner(coeffs, orb_ref, rot_ref, rotated_ref, full)
     for c in copies:
         c.wait_send()
 
 
-def exchange(packed, scale):
+def exchange(packed, orbitals, rotation, scale, coeffs):
     size = lax.axis_size("row")
     rows, width = packed.shape
     steps = size.bit_length() - 1
     tracks = max(1, min(TRACKS, rows // (16 * size)))
     return pl.pallas_call(
-        functools.partial(exchange_kernel, tracks, scale),
-        out_shape=jax.ShapeDtypeStruct((rows, width), jnp.bfloat16),
-        in_specs=[pl.BlockSpec(memory_space=pltpu.VMEM)],
+        functools.partial(exchange_kernel, tracks, scale, coeffs),
+        out_shape=jax.ShapeDtypeStruct(orbitals.shape, jnp.bfloat16),
+        in_specs=[pl.BlockSpec(memory_space=pltpu.VMEM)] * 3,
         out_specs=pl.BlockSpec(memory_space=pltpu.VMEM),
         scratch_shapes=[
             pltpu.VMEM((rows, width), SENT),
             pltpu.VMEM((rows // 2, width), jnp.float32),
             pltpu.VMEM((rows // 2, width), SENT),
+            pltpu.VMEM((rows, width), jnp.bfloat16),
+            pltpu.VMEM((rows, rows), jnp.bfloat16),
             pltpu.SemaphoreType.DMA((tracks, 2 * steps)),
             pltpu.SemaphoreType.DMA((tracks, 2 * steps)),
         ],
         compiler_params=pltpu.CompilerParams(
-            collective_id=0, has_side_effects=True, vmem_limit_bytes=48 * 2**20
+            collective_id=0, has_side_effects=True, vmem_limit_bytes=56 * 2**20
         ),
-    )(packed)
+    )(packed, orbitals, rotation)
 
 
 def shards(orbitals, rotation, fock_tiles, fock_pattern, correlation_tiles, correlation_pattern):
@@ -235,16 +247,9 @@
         compiler_params=pltpu.CompilerParams(vmem_limit_bytes=40 * 2**20),
     )(rotation, applied)
 
-    gram_low = exchange(packed, 4.0 / basis_total)
-
-    rotated = pl.pallas_call(
-        functools.partial(horner_kernel, half, (cos_coeffs, sin_coeffs)),
-        out_shape=jax.ShapeDtypeStruct((local_rows, orbital_count), jnp.bfloat16),
-        in_specs=[pl.BlockSpec(memory_space=pltpu.VMEM)] * 3,
-        out_specs=pl.BlockSpec(memory_space=pltpu.VMEM),
-        scratch_shapes=[pltpu.VMEM((orbital_count, orbital_count), jnp.bfloat16)],
-        compiler_params=pltpu.CompilerParams(vmem_limit_bytes=48 * 2**20),
-    )(gram_low, orbitals, rotation)
+    rotated = exchange(
+        packed, orbitals, rotation, 4.0 / basis_total, (cos_coeffs, sin_coeffs)
+    )
     rotated_ext = halo(rotated, 2 * tile_size)
     fock_rotated = near_product(fock_tiles, fock_pattern, rotated_ext, blocks_dev, tile_size)
     return (rotated, fock_rotated)

time: 158 us -> 151 us (0.956)
  Pallas kernels: 88.3 us -> 83.7 us
    pallas_call x2 -> x1, Pallas kernels: 86.7 us -> 82.2 us  [exchange(): pl.pallas_call(functools.partial(exchange_kernel, tracks, scale, coeffs),...]
    unnamed x12 -> x11, local copies, waits for them, and re-layouts: 8.04 us -> 6.89 us
where the time goes in v3:
time: 151 us; the launch traced here: 149 us
  Pallas kernels  83.7 us (55%)
  waiting for transfers between devices  40.1 us (27%)
  starting transfers between devices  11.3 us (7%)
  local copies, waits for them, and re-layouts  7 us (5%)
  other arithmetic  3.84 us (3%)
  matrix products  2.42 us (2%)
    pallas_call x1, Pallas kernels, exchange(): pl.pallas_call(functools.partial(exchange_kernel, tracks, scale, coeffs),...  82.2 us
    ppermute x2, waiting for transfers between devices, halo(): after = lax.ppermute(value[:width], 'row', down)  33.2 us
    ppermute x2, starting transfers between devices, halo(): before = lax.ppermute(value[length - width:], 'row', up)  7.16 us
    unnamed x11, local copies, waits for them, and re-layouts  6.89 us
    ppermute x2, waiting for transfers between devices, halo(): before = lax.ppermute(value[length - width:], 'row', up)  6.85 us
    ppermute x2, starting transfers between devices, halo(): after = lax.ppermute(value[:width], 'row', down)  4.17 us
  transfers between devices with their start and end apart: 4, of which 3 were waited for; matrix products, arithmetic and copies ran while one was open for 3% of the time, Pallas kernels for 0%

profile of v3, /device:TPU:25, one launch (start us, length us, event | category | flops | bytes accessed | tf_op | source)
XLA Modules:
  0.0 149.2 jit_solution(16777776757858450818)
XLA Ops:
  0.6 0.0 copy-start.1
  0.6 3.8 %collective-permute-start = (bf16[256,2048]{1,0:T(8,128)(2,1)}, bf16[256,2048]{1,0:T(8,128)(2,1)}, u32[]{:S(2)}, u32[]{:S(2)}) collective-permute-start(bf16[256,2048]{1,0:T(8,128)(2,1)} %rot_ref.3), channel_id=1, source_target_pairs={{0,1},{1,2},{2,3},{3,4},{4,5},{5,6},{6,7},{7,8},{8,9},{9,10},{10,1... | collective-permute-start | bytes 3145736 | tf_op jit(solution)/shard_map/ppermute | solution.py:21
  4.5 1.9 %collective-permute-start.1 = (bf16[256,2048]{1,0:T(8,128)(2,1)}, bf16[256,2048]{1,0:T(8,128)(2,1)S(1)}, u32[]{:S(2)}, u32[]{:S(2)}) collective-permute-start(bf16[256,2048]{1,0:T(8,128)(2,1)} %rot_ref.3), channel_id=1, source_target_pairs={{1,0},{2,1},{3,2},{4,3},{5,4},{6,5},{7,6},{8,7},{9,8},{10,9},{11,1... | collective-permute-start | bytes 3145736 | tf_op jit(solution)/shard_map/ppermute | solution.py:22
  6.4 0.7 compare_or_fusion
  7.1 1.2 copy.9
  8.3 1.2 copy.8
  9.5 0.1 broadcast_select_fusion
  9.7 6.8 %collective-permute-done = bf16[256,2048]{1,0:T(8,128)(2,1)} collective-permute-done((bf16[256,2048]{1,0:T(8,128)(2,1)}, bf16[256,2048]{1,0:T(8,128)(2,1)}, u32[]{:S(2)}, u32[]{:S(2)}) %collective-permute-start) | collective-permute-done | bytes 1048608 | tf_op jit(solution)/shard_map/ppermute | solution.py:21
  16.5 1.3 constant_dynamic-update-slice_fusion.2
  17.9 0.0 copy-done.1
  17.9 0.1 constant_dynamic-update-slice_fusion.1
  17.9 11.3 %collective-permute-done.1 = bf16[256,2048]{1,0:T(8,128)(2,1)S(1)} collective-permute-done((bf16[256,2048]{1,0:T(8,128)(2,1)}, bf16[256,2048]{1,0:T(8,128)(2,1)S(1)}, u32[]{:S(2)}, u32[]{:S(2)}) %collective-permute-start.1) | collective-permute-done | bytes 1048608 | tf_op jit(solution)/shard_map/ppermute | solution.py:22
  29.2 0.1 constant_dynamic-update-slice_fusion
  29.3 0.6 fusion.11
  29.9 0.6 fusion.8
  30.5 0.1 pad_maximum_fusion.2.app_ref
  30.6 1.6 %shard_map.77.packed_ref = bf16[2048,1152]{1,0:T(8,128)(2,1)S(1)} custom-call(bf16[256,2048]{1,0:T(8,128)(2,1)S(1)} %copy-done.1, bf16[256,2048]{1,0:T(8,128)(2,1)S(1)} %pad_maximum_fusion.2.app_ref), custom_call_target="tpu_custom_call" | custom-call | tf_op jit(solution)/shard_map/pallas_call | solution.py:242
  32.2 0.0 copy-start
  32.2 2.1 %copy-done = bf16[2048,1152]{1,0:T(8,128)(2,1)} copy-done((bf16[2048,1152]{1,0:T(8,128)(2,1)}, bf16[2048,1152]{1,0:T(8,128)(2,1)S(1)}, u32[]{:S(2)}) %copy-start) | copy-done | bytes 4718616
  34.3 82.2 %shard_map.78 = bf16[256,2048]{1,0:T(8,128)(2,1)} custom-call(bf16[2048,1152]{1,0:T(8,128)(2,1)} %copy-done, bf16[256,2048]{1,0:T(8,128)(2,1)} %orb_ref.1, bf16[256,2048]{1,0:T(8,128)(2,1)} %rot_ref.3), custom_call_target="tpu_custom_call" | custom-call | tf_op jit(solution)/shard_map/pallas_call | solution.py:208
  116.5 2.2 %collective-permute-start.3 = (bf16[256,2048]{1,0:T(8,128)(2,1)}, bf16[256,2048]{1,0:T(8,128)(2,1)S(1)}, u32[]{:S(2)}, u32[]{:S(2)}) collective-permute-start(bf16[256,2048]{1,0:T(8,128)(2,1)} %shard_map.78), channel_id=1, source_target_pairs={{1,0},{2,1},{3,2},{4,3},{5,4},{6,5},{7,6},{8,7},{9,8},{10,9},{11,1... | collective-permute-start | bytes 3145736 | tf_op jit(solution)/shard_map/ppermute | solution.py:22
  118.8 3.3 %collective-permute-start.2 = (bf16[256,2048]{1,0:T(8,128)(2,1)}, bf16[256,2048]{1,0:T(8,128)(2,1)S(1)}, u32[]{:S(2)}, u32[]{:S(2)}) collective-permute-start(bf16[256,2048]{1,0:T(8,128)(2,1)} %shard_map.78), channel_id=1, source_target_pairs={{0,1},{1,2},{2,3},{3,4},{4,5},{5,6},{6,7},{7,8},{8,9},{9,10},{10,1... | collective-permute-start | bytes 3145736 | tf_op jit(solution)/shard_map/ppermute | solution.py:21
  122.1 22.0 %collective-permute-done.3 = bf16[256,2048]{1,0:T(8,128)(2,1)S(1)} collective-permute-done((bf16[256,2048]{1,0:T(8,128)(2,1)}, bf16[256,2048]{1,0:T(8,128)(2,1)S(1)}, u32[]{:S(2)}, u32[]{:S(2)}) %collective-permute-start.3) | collective-permute-done | bytes 1048608 | tf_op jit(solution)/shard_map/ppermute | solution.py:22
  144.1 0.0 collective-permute-done.2
  144.1 1.4 pad_maximum_fusion
  145.5 0.6 fusion
  146.2 0.0 copy-start.2
  146.2 0.6 fusion.2
  146.8 1.5 pad_maximum_fusion.1
  148.2 0.0 copy-done.2
  148.2 1.0 copy.13
  (3 shorter events, 0.1 us)
Async XLA Ops:
  0.6 17.2 %copy-start.1 = (bf16[256,2048]{1,0:T(8,128)(2,1)S(1)}, bf16[256,2048]{1,0:T(8,128)(2,1)}, u32[]{:S(2)}) copy-start(bf16[256,2048]{1,0:T(8,128)(2,1)} %rot_ref.3) | copy-start | bytes 3145732
  0.6 15.9 %collective-permute-start = (bf16[256,2048]{1,0:T(8,128)(2,1)}, bf16[256,2048]{1,0:T(8,128)(2,1)}, u32[]{:S(2)}, u32[]{:S(2)}) collective-permute-start(bf16[256,2048]{1,0:T(8,128)(2,1)} %rot_ref.3), channel_id=1, source_target_pairs={{0,1},{1,2},{2,3},{3,4},{4,5},{5,6},{6,7},{7,8},{8,9},{9,10},{10,1... | collective-permute-start | bytes 3145736 | tf_op jit(solution)/shard_map/ppermute | solution.py:21
  4.5 24.7 %collective-permute-start.1 = (bf16[256,2048]{1,0:T(8,128)(2,1)}, bf16[256,2048]{1,0:T(8,128)(2,1)S(1)}, u32[]{:S(2)}, u32[]{:S(2)}) collective-permute-start(bf16[256,2048]{1,0:T(8,128)(2,1)} %rot_ref.3), channel_id=1, source_target_pairs={{1,0},{2,1},{3,2},{4,3},{5,4},{6,5},{7,6},{8,7},{9,8},{10,9},{11,1... | collective-permute-start | bytes 3145736 | tf_op jit(solution)/shard_map/ppermute | solution.py:22
  32.2 2.1 %copy-start = (bf16[2048,1152]{1,0:T(8,128)(2,1)}, bf16[2048,1152]{1,0:T(8,128)(2,1)S(1)}, u32[]{:S(2)}) copy-start(bf16[2048,1152]{1,0:T(8,128)(2,1)S(1)} %shard_map.77.packed_ref) | copy-start | bytes 14155780
  116.5 27.6 %collective-permute-start.3 = (bf16[256,2048]{1,0:T(8,128)(2,1)}, bf16[256,2048]{1,0:T(8,128)(2,1)S(1)}, u32[]{:S(2)}, u32[]{:S(2)}) collective-permute-start(bf16[256,2048]{1,0:T(8,128)(2,1)} %shard_map.78), channel_id=1, source_target_pairs={{1,0},{2,1},{3,2},{4,3},{5,4},{6,5},{7,6},{8,7},{9,8},{10,9},{11,1... | collective-permute-start | bytes 3145736 | tf_op jit(solution)/shard_map/ppermute | solution.py:22
  118.8 25.3 %collective-permute-start.2 = (bf16[256,2048]{1,0:T(8,128)(2,1)}, bf16[256,2048]{1,0:T(8,128)(2,1)S(1)}, u32[]{:S(2)}, u32[]{:S(2)}) collective-permute-start(bf16[256,2048]{1,0:T(8,128)(2,1)} %shard_map.78), channel_id=1, source_target_pairs={{0,1},{1,2},{2,3},{3,4},{4,5},{5,6},{6,7},{7,8},{8,9},{9,10},{10,1... | collective-permute-start | bytes 3145736 | tf_op jit(solution)/shard_map/ppermute | solution.py:21
  146.2 2.1 %copy-start.2 = (bf16[256,2048]{1,0:T(8,128)(2,1)S(1)}, bf16[256,2048]{1,0:T(8,128)(2,1)}, u32[]{:S(2)}) copy-start(bf16[256,2048]{1,0:T(8,128)(2,1)} %shard_map.78) | copy-start | bytes 3145732

commit v4 on v3

--- a/solution.py
+++ b/solution.py
@@ -12,6 +12,7 @@
 BLOCK = 128
 SENT = jnp.bfloat16
 TRACKS = 8
+CHUNK = 512
 
 
 def halo(value, width):
@@ -23,18 +24,26 @@
     return jnp.concatenate([before, value, after], axis=0)
 
 
-def near_product(tile_values, pattern, extended, blocks_dev, tile_size):
-    orbital_count = extended.shape[1]
-    blocks = extended.reshape(blocks_dev + 4, tile_size, orbital_count)
+def wide_tiles(tile_values, pattern):
+    blocks_dev, slots, tile_size, _ = tile_values.shape
     slot_ids = lax.broadcasted_iota(jnp.int32, pattern.shape, 1)
     live_mask = (pattern > 0) | (slot_ids == 2)
     masked = jnp.where(live_mask[:, :, None, None], tile_values, jnp.zeros((), jnp.bfloat16))
-    outs = []
-    for b in range(blocks_dev):
-        wide = jnp.swapaxes(masked[b], 0, 1).reshape(tile_size, 5 * tile_size)
-        field = blocks[b : b + 5].reshape(5 * tile_size, orbital_count)
-        outs.append(jnp.dot(wide, field, preferred_element_type=jnp.float32))
-    return jnp.concatenate(outs, axis=0)
+    return jnp.swapaxes(masked, 1, 2).reshape(blocks_dev * tile_size, slots * tile_size)
+
+
+def near_product(wide, extended):
+    return jnp.concatenate(
+        [
+            jnp.dot(
+                wide[at : at + BLOCK],
+                extended[at : at + 5 * BLOCK],
+                preferred_element_type=jnp.float32,
+            )
+            for at in range(0, wide.shape[0], BLOCK)
+        ],
+        axis=0,
+    )
 
 
 def gram_kernel(half, rot_ref, app_ref, out_ref):
@@ -68,28 +77,28 @@
                 full[j * BLOCK : (j + 1) * BLOCK, i * BLOCK : (i + 1) * BLOCK] = tile.T
 
 
-def horner(coeffs, orb_ref, rot_ref, out_ref, full):
+def horner(coeffs, orb_ref, rot_ref, full, columns, emit):
     cos_coeffs, sin_coeffs = coeffs
     orb = orb_ref[...].astype(jnp.float32)
     rot = rot_ref[...].astype(jnp.float32)
     current = (cos_coeffs[ORDER] * orb + sin_coeffs[ORDER] * rot).astype(jnp.bfloat16)
-    columns = 512
     for degree in range(ORDER - 1, -1, -1):
         parts = []
         for c in range(0, orb_ref.shape[1], columns):
             total = jnp.dot(current, full[:, c : c + columns], preferred_element_type=jnp.float32)
             o = orb_ref[:, c : c + columns].astype(jnp.float32)
             r = rot_ref[:, c : c + columns].astype(jnp.float32)
-            parts.append(
-                (total + cos_coeffs[degree] * o + sin_coeffs[degree] * r).astype(jnp.bfloat16)
-            )
-        current = jnp.concatenate(parts, axis=1)
-    out_ref[...] = current
+            part = (total + cos_coeffs[degree] * o + sin_coeffs[degree] * r).astype(jnp.bfloat16)
+            if degree == 0:
+                emit(c, part)
+            parts.append(part)
+        if degree:
+            current = jnp.concatenate(parts, axis=1)
 
 
 def exchange_kernel(
-    tracks, scale, coeffs, packed_ref, orb_ref, rot_ref, rotated_ref,
-    got, acc, send, out_ref, full, send_sem, recv_sem,
+    tracks, scale, coeffs, packed_ref, orb_ref, rot_ref, wide_ref, rotated_ref, fock_ref,
+    got, acc, send, out_ref, full, ext, send_sem, recv_sem, halo_send, halo_recv,
 ):
     size = lax.axis_size("row")
     me = lax.axis_index("row")
@@ -125,7 +134,32 @@
         pl.semaphore_signal(
             barrier, inc=1, device_id={"row": partner(1 << b)}, device_id_type=pl.DeviceIdType.MESH
         )
-    pl.semaphore_wait(barrier, steps)
+    below, above = me > 0, me < size - 1
+    inner = jnp.logical_and(below, above)
+
+    @pl.when(inner)
+    def _():
+        pl.semaphore_signal(
+            barrier,
+            inc=1,
+            device_id={"row": me - 1 + 2 * lax.rem(me, 2)},
+            device_id_type=pl.DeviceIdType.MESH,
+        )
+        pl.semaphore_wait(barrier, steps + 1)
+
+    @pl.when(jnp.logical_not(inner))
+    def _():
+        pl.semaphore_wait(barrier, steps)
+
+    local, wing = orb_ref.shape[0], 2 * BLOCK
+
+    @pl.when(me == 0)
+    def _():
+        ext[:wing, :] = jnp.zeros((wing, ext.shape[1]), ext.dtype)
+
+    @pl.when(me == size - 1)
+    def _():
+        ext[local + wing :, :] = jnp.zeros((wing, ext.shape[1]), ext.dtype)
 
     copies = []
     pending = []
@@ -195,38 +229,86 @@
             else:
                 spread(out_ref, full, t * rows // BLOCK, (t + 1) * rows // BLOCK)
         count = 2 * count
-    horner(coeffs, orb_ref, rot_ref, rotated_ref, full)
+
+    columns = CHUNK
+
+    def halo_copy(side, c):
+        source, target, index = ((wing, local + wing, me - 1), (local, 0, me + 1))[side]
+        return pltpu.make_async_remote_copy(
+            src_ref=ext.at[pl.ds(source, wing), pl.ds(c, columns)],
+            dst_ref=ext.at[pl.ds(target, wing), pl.ds(c, columns)],
+            send_sem=halo_send.at[side, c // columns],
+            recv_sem=halo_recv.at[side, c // columns],
+            device_id={"row": index},
+            device_id_type=pl.DeviceIdType.MESH,
+        )
+
+    def emit(c, part):
+        rotated_ref[:, c : c + columns] = part
+        ext[wing : wing + local, c : c + columns] = part
+        for side, there in ((0, below), (1, above)):
+
+            @pl.when(there)
+            def _():
+                halo_copy(side, c).start()
+
+    horner(coeffs, orb_ref, rot_ref, full, columns, emit)
+    for c in range(0, orb_ref.shape[1], columns):
+        for side, there in ((0, above), (1, below)):
+
+            @pl.when(there)
+            def _():
+                halo_copy(side, c).wait_recv()
+
+        for at in range(0, local, BLOCK):
+            fock_ref[at : at + BLOCK, c : c + columns] = jnp.dot(
+                wide_ref[at : at + BLOCK, :],
+                ext[at : at + 5 * BLOCK, c : c + columns],
+                preferred_element_type=jnp.float32,
+            )
+    for c in range(0, orb_ref.shape[1], columns):
+        for side, there in ((0, below), (1, above)):
+
+            @pl.when(there)
+            def _():
+                halo_copy(side, c).wait_send()
+
     for c in copies:
         c.wait_send()
 
 
-def exchange(packed, orbitals, rotation, scale, coeffs):
+def exchange(packed, orbitals, rotation, wide, scale, coeffs):
     size = lax.axis_size("row")
     rows, width = packed.shape
     steps = size.bit_length() - 1
     tracks = max(1, min(TRACKS, rows // (16 * size)))
     return pl.pallas_call(
         functools.partial(exchange_kernel, tracks, scale, coeffs),
-        out_shape=jax.ShapeDtypeStruct(orbitals.shape, jnp.bfloat16),
-        in_specs=[pl.BlockSpec(memory_space=pltpu.VMEM)] * 3,
-        out_specs=pl.BlockSpec(memory_space=pltpu.VMEM),
+        out_shape=(
+            jax.ShapeDtypeStruct(orbitals.shape, jnp.bfloat16),
+            jax.ShapeDtypeStruct(orbitals.shape, jnp.float32),
+        ),
+        in_specs=[pl.BlockSpec(memory_space=pltpu.VMEM)] * 4,
+        out_specs=(pl.BlockSpec(memory_space=pltpu.VMEM),) * 2,
         scratch_shapes=[
             pltpu.VMEM((rows, width), SENT),
             pltpu.VMEM((rows // 2, width), jnp.float32),
             pltpu.VMEM((rows // 2, width), SENT),
             pltpu.VMEM((rows, width), jnp.bfloat16),
             pltpu.VMEM((rows, rows), jnp.bfloat16),
+            pltpu.VMEM((orbitals.shape[0] + 4 * BLOCK, rows), jnp.bfloat16),
             pltpu.SemaphoreType.DMA((tracks, 2 * steps)),
             pltpu.SemaphoreType.DMA((tracks, 2 * steps)),
+            pltpu.SemaphoreType.DMA((2, rows // CHUNK)),
+            pltpu.SemaphoreType.DMA((2, rows // CHUNK)),
         ],
         compiler_params=pltpu.CompilerParams(
             collective_id=0, has_side_effects=True, vmem_limit_bytes=56 * 2**20
         ),
-    )(packed, orbitals, rotation)
+    )(packed, orbitals, rotation, wide)
 
 
 def shards(orbitals, rotation, fock_tiles, fock_pattern, correlation_tiles, correlation_pattern):
-    blocks_dev = correlation_tiles.shape[0]
     tile_size = correlation_tiles.shape[2]
     local_rows, orbital_count = rotation.shape
     size = lax.axis_size("row")
@@ -236,9 +318,8 @@
     cos_coeffs = [(-1.0) ** degree / math.factorial(2 * degree) for degree in range(ORDER + 1)]
     sin_coeffs = [(-1.0) ** degree / math.factorial(2 * degree + 1) for degree in range(ORDER + 1)]
     extended = halo(rotation, 2 * tile_size)
-    applied = near_product(
-        correlation_tiles, correlation_pattern, extended, blocks_dev, tile_size
-    ).astype(jnp.bfloat16)
+    applied = near_product(wide_tiles(correlation_tiles, correlation_pattern), extended)
+    applied = applied.astype(jnp.bfloat16)
     packed = pl.pallas_call(
         functools.partial(gram_kernel, half),
         out_shape=jax.ShapeDtypeStruct((orbital_count, width), SENT),
@@ -247,12 +328,10 @@
         compiler_params=pltpu.CompilerParams(vmem_limit_bytes=40 * 2**20),
     )(rotation, applied)
 
-    rotated = exchange(
-        packed, orbitals, rotation, 4.0 / basis_total, (cos_coeffs, sin_coeffs)
+    wide = wide_tiles(fock_tiles, fock_pattern)
+    return exchange(
+        packed, orbitals, rotation, wide, 4.0 / basis_total, (cos_coeffs, sin_coeffs)
     )
-    rotated_ext = halo(rotated, 2 * tile_size)
-    fock_rotated = near_product(fock_tiles, fock_pattern, rotated_ext, blocks_dev, tile_size)
-    return (rotated, fock_rotated)
 
 
 def solution(mesh):

time: 151 us -> 146 us (0.967)
  Pallas kernels: 83.7 us -> 107 us
  waiting for transfers between devices: 40.1 us -> 17.1 us
  starting transfers between devices: 11.3 us -> 5.64 us
  local copies, waits for them, and re-layouts: 7 us -> 12.2 us
  other arithmetic: 3.84 us -> 0.93 us
    pallas_call x1, Pallas kernels: 82.2 us -> 105 us  [exchange(): pl.pallas_call(functools.partial(exchange_kernel, tracks, scale, coeffs),...]
    ppermute x2 -> x1, waiting for transfers between devices: 33.2 us -> 11.4 us  [halo(): after = lax.ppermute(value[:width], 'row', down)]
    unnamed x11 -> x13, local copies, waits for them, and re-layouts: 6.89 us -> 10.5 us
    ppermute x2 -> x1, starting transfers between devices: 7.16 us -> 3.71 us  [halo(): before = lax.ppermute(value[length - width:], 'row', up)]
    concatenate x3 -> x1, other arithmetic: 3.01 us -> 0.1 us  [near_product(): jnp.concatenate([jnp.dot(wide[at:at + BLOCK], extended[at:at + 5 * BLOCK]...]
    ppermute x2 -> x1, starting transfers between devices: 4.17 us -> 1.92 us  [halo(): after = lax.ppermute(value[:width], 'row', down)]
    ppermute x2 -> x1, waiting for transfers between devices: 6.85 us -> 5.67 us  [halo(): before = lax.ppermute(value[length - width:], 'row', up)]
  transfers between devices with their start and end apart: 4 -> 2, of which waited for: 3 -> 2; matrix products, arithmetic and copies ran while one was open for 3% -> 4% of each run, Pallas kernels for 0% -> 0%
where the time goes in v4:
time: 146 us; the launch traced here: 145 us
  Pallas kernels  107 us (73%)
  waiting for transfers between devices  17.1 us (12%)
  local copies, waits for them, and re-layouts  12.2 us (8%)
  starting transfers between devices  5.64 us (4%)
    pallas_call x1, Pallas kernels, exchange(): pl.pallas_call(functools.partial(exchange_kernel, tracks, scale, coeffs),...  105 us
    ppermute x1, waiting for transfers between devices, halo(): after = lax.ppermute(value[:width], 'row', down)  11.4 us
    unnamed x13, local copies, waits for them, and re-layouts  10.5 us
    ppermute x1, waiting for transfers between devices, halo(): before = lax.ppermute(value[length - width:], 'row', up)  5.67 us
    ppermute x1, starting transfers between devices, halo(): before = lax.ppermute(value[length - width:], 'row', up)  3.71 us
  transfers between devices with their start and end apart: 2, of which 2 were waited for; matrix products, arithmetic and copies ran while one was open for 4% of the time, Pallas kernels for 0%

profile of v4, /device:TPU:25, one launch (start us, length us, event | category | flops | bytes accessed | tf_op | source)
XLA Modules:
  0.0 144.6 jit_solution(7318946911529211136)
XLA Ops:
  0.6 3.7 %collective-permute-start = (bf16[256,2048]{1,0:T(8,128)(2,1)}, bf16[256,2048]{1,0:T(8,128)(2,1)}, u32[]{:S(2)}, u32[]{:S(2)}) collective-permute-start(bf16[256,2048]{1,0:T(8,128)(2,1)} %rot_ref.3), channel_id=1, source_target_pairs={{0,1},{1,2},{2,3},{3,4},{4,5},{5,6},{6,7},{7,8},{8,9},{9,10},{10,1... | collective-permute-start | bytes 3145736 | tf_op jit(solution)/shard_map/ppermute | solution.py:22
  4.3 1.9 %collective-permute-start.1 = (bf16[256,2048]{1,0:T(8,128)(2,1)}, bf16[256,2048]{1,0:T(8,128)(2,1)}, u32[]{:S(2)}, u32[]{:S(2)}) collective-permute-start(bf16[256,2048]{1,0:T(8,128)(2,1)} %rot_ref.3), channel_id=1, source_target_pairs={{1,0},{2,1},{3,2},{4,3},{5,4},{6,5},{7,6},{8,7},{9,8},{10,9},{11,1... | collective-permute-start | bytes 3145736 | tf_op jit(solution)/shard_map/ppermute | solution.py:23
  6.3 0.7 compare_or_fusion
  7.0 1.2 copy.10
  8.2 0.0 copy-start.1
  8.2 1.3 copy.9
  9.5 0.1 select_bitcast_fusion
  9.6 0.3 copy.13
  9.9 0.8 copy.17
  10.7 5.7 %collective-permute-done = bf16[256,2048]{1,0:T(8,128)(2,1)} collective-permute-done((bf16[256,2048]{1,0:T(8,128)(2,1)}, bf16[256,2048]{1,0:T(8,128)(2,1)}, u32[]{:S(2)}, u32[]{:S(2)}) %collective-permute-start) | collective-permute-done | bytes 1048608 | tf_op jit(solution)/shard_map/ppermute | solution.py:22
  16.4 1.3 constant_dynamic-update-slice_fusion.2
  17.7 0.0 copy-done.1
  17.7 0.1 constant_dynamic-update-slice_fusion.1
  17.8 11.4 %collective-permute-done.1 = bf16[256,2048]{1,0:T(8,128)(2,1)} collective-permute-done((bf16[256,2048]{1,0:T(8,128)(2,1)}, bf16[256,2048]{1,0:T(8,128)(2,1)}, u32[]{:S(2)}, u32[]{:S(2)}) %collective-permute-start.1) | collective-permute-done | bytes 1048608 | tf_op jit(solution)/shard_map/ppermute | solution.py:23
  29.2 1.3 constant_dynamic-update-slice_fusion
  30.5 0.6 fusion.7
  31.1 0.6 fusion.4
  31.7 0.1 pad_maximum_fusion.app_ref
  31.8 1.6 %shard_map.77.packed_ref = bf16[2048,1152]{1,0:T(8,128)(2,1)S(1)} custom-call(bf16[256,2048]{1,0:T(8,128)(2,1)S(1)} %copy-done.1, bf16[256,2048]{1,0:T(8,128)(2,1)S(1)} %pad_maximum_fusion.app_ref), custom_call_target="tpu_custom_call" | custom-call | tf_op jit(solution)/shard_map/pallas_call | solution.py:323
  33.4 0.0 copy-start
  33.4 2.1 %copy-done = bf16[2048,1152]{1,0:T(8,128)(2,1)} copy-done((bf16[2048,1152]{1,0:T(8,128)(2,1)}, bf16[2048,1152]{1,0:T(8,128)(2,1)S(1)}, u32[]{:S(2)}) %copy-start) | copy-done | bytes 4718616
  35.6 105.2 %shard_map.78 = (bf16[256,2048]{1,0:T(8,128)(2,1)}, f32[256,2048]{1,0:T(8,128)}) custom-call(bf16[2048,1152]{1,0:T(8,128)(2,1)} %copy-done, bf16[256,2048]{1,0:T(8,128)(2,1)} %orb_ref.1, bf16[256,2048]{1,0:T(8,128)(2,1)} %rot_ref.3, bf16[256,640]{1,0:T(8,128)(2,1)} %bitcast.14), custom_call_target="tpu_custom_call" | custom-call | tf_op jit(solution)/shard_map/pallas_call | solution.py:285
  140.8 0.0 copy-start.2
  140.8 2.5 %copy.22 = bf16[256,2048]{1,0:T(8,128)(2,1)} copy(bf16[256,2048]{1,0:T(8,128)(2,1)} %get-tuple-element.10) | data formatting | bytes 2097152
  143.3 0.0 copy-done.2
  143.3 1.3 copy.23
  (2 shorter events, 0.0 us)
Async XLA Ops:
  0.6 15.8 %collective-permute-start = (bf16[256,2048]{1,0:T(8,128)(2,1)}, bf16[256,2048]{1,0:T(8,128)(2,1)}, u32[]{:S(2)}, u32[]{:S(2)}) collective-permute-start(bf16[256,2048]{1,0:T(8,128)(2,1)} %rot_ref.3), channel_id=1, source_target_pairs={{0,1},{1,2},{2,3},{3,4},{4,5},{5,6},{6,7},{7,8},{8,9},{9,10},{10,1... | collective-permute-start | bytes 3145736 | tf_op jit(solution)/shard_map/ppermute | solution.py:22
  4.3 24.8 %collective-permute-start.1 = (bf16[256,2048]{1,0:T(8,128)(2,1)}, bf16[256,2048]{1,0:T(8,128)(2,1)}, u32[]{:S(2)}, u32[]{:S(2)}) collective-permute-start(bf16[256,2048]{1,0:T(8,128)(2,1)} %rot_ref.3), channel_id=1, source_target_pairs={{1,0},{2,1},{3,2},{4,3},{5,4},{6,5},{7,6},{8,7},{9,8},{10,9},{11,1... | collective-permute-start | bytes 3145736 | tf_op jit(solution)/shard_map/ppermute | solution.py:23
  8.2 9.5 %copy-start.1 = (bf16[256,2048]{1,0:T(8,128)(2,1)S(1)}, bf16[256,2048]{1,0:T(8,128)(2,1)}, u32[]{:S(2)}) copy-start(bf16[256,2048]{1,0:T(8,128)(2,1)} %rot_ref.3) | copy-start | bytes 3145732
  33.4 2.1 %copy-start = (bf16[2048,1152]{1,0:T(8,128)(2,1)}, bf16[2048,1152]{1,0:T(8,128)(2,1)S(1)}, u32[]{:S(2)}) copy-start(bf16[2048,1152]{1,0:T(8,128)(2,1)S(1)} %shard_map.77.packed_ref) | copy-start | bytes 14155780
  140.8 2.5 %copy-start.2 = (f32[256,2048]{1,0:T(8,128)S(1)}, f32[256,2048]{1,0:T(8,128)}, u32[]{:S(2)}) copy-start(f32[256,2048]{1,0:T(8,128)} %get-tuple-element.11) | copy-start | bytes 6291460

commit v5 on v4

--- a/solution.py
+++ b/solution.py
@@ -108,7 +108,8 @@
     half = rows // 2
     outer = [1 << b for b in range(1, steps)]
     swapped = [outer[1], outer[0]] + outer[2:] if len(outer) > 1 else outer
-    orders = [[1] + (outer if t % 2 == 0 else swapped) for t in range(tracks)]
+    third = outer[2:3] + outer[:2] + outer[3:]
+    orders = [[1] + (outer, swapped, third)[t % 3] for t in range(tracks)]
 
     def high(bit):
         return lax.rem(me // bit, 2)

time: 146 us -> 146 us (level)
  no operation moved by 1% of the time
where the time goes in v5:
time: 146 us; the launch traced here: 143 us
  Pallas kernels  106 us (73%)
  waiting for transfers between devices  17.1 us (12%)
  local copies, waits for them, and re-layouts  12.2 us (8%)
  starting transfers between devices  5.64 us (4%)
    pallas_call x1, Pallas kernels, exchange(): pl.pallas_call(functools.partial(exchange_kernel, tracks, scale, coeffs),...  104 us
    ppermute x1, waiting for transfers between devices, halo(): after = lax.ppermute(value[:width], 'row', down)  11.4 us
    unnamed x13, local copies, waits for them, and re-layouts  10.5 us
    ppermute x1, waiting for transfers between devices, halo(): before = lax.ppermute(value[length - width:], 'row', up)  5.67 us
    ppermute x1, starting transfers between devices, halo(): before = lax.ppermute(value[length - width:], 'row', up)  3.71 us
  transfers between devices with their start and end apart: 2, of which 2 were waited for; matrix products, arithmetic and copies ran while one was open for 4% of the time, Pallas kernels for 0%

profile of v5, /device:TPU:25, one launch (start us, length us, event | category | flops | bytes accessed | tf_op | source)
XLA Modules:
  0.0 143.4 jit_solution(3927221966967671658)
XLA Ops:
  0.6 3.7 %collective-permute-start = (bf16[256,2048]{1,0:T(8,128)(2,1)}, bf16[256,2048]{1,0:T(8,128)(2,1)}, u32[]{:S(2)}, u32[]{:S(2)}) collective-permute-start(bf16[256,2048]{1,0:T(8,128)(2,1)} %rot_ref.3), channel_id=1, source_target_pairs={{0,1},{1,2},{2,3},{3,4},{4,5},{5,6},{6,7},{7,8},{8,9},{9,10},{10,1... | collective-permute-start | bytes 3145736 | tf_op jit(solution)/shard_map/ppermute | solution.py:22
  4.3 1.9 %collective-permute-start.1 = (bf16[256,2048]{1,0:T(8,128)(2,1)}, bf16[256,2048]{1,0:T(8,128)(2,1)}, u32[]{:S(2)}, u32[]{:S(2)}) collective-permute-start(bf16[256,2048]{1,0:T(8,128)(2,1)} %rot_ref.3), channel_id=1, source_target_pairs={{1,0},{2,1},{3,2},{4,3},{5,4},{6,5},{7,6},{8,7},{9,8},{10,9},{11,1... | collective-permute-start | bytes 3145736 | tf_op jit(solution)/shard_map/ppermute | solution.py:23
  6.3 0.7 compare_or_fusion
  7.0 1.2 copy.10
  8.2 0.0 copy-start.1
  8.2 1.3 copy.9
  9.5 0.1 select_bitcast_fusion
  9.6 0.3 copy.13
  9.9 0.8 copy.17
  10.7 5.7 %collective-permute-done = bf16[256,2048]{1,0:T(8,128)(2,1)} collective-permute-done((bf16[256,2048]{1,0:T(8,128)(2,1)}, bf16[256,2048]{1,0:T(8,128)(2,1)}, u32[]{:S(2)}, u32[]{:S(2)}) %collective-permute-start) | collective-permute-done | bytes 1048608 | tf_op jit(solution)/shard_map/ppermute | solution.py:22
  16.4 1.3 constant_dynamic-update-slice_fusion.2
  17.7 0.0 copy-done.1
  17.7 0.1 constant_dynamic-update-slice_fusion.1
  17.8 11.4 %collective-permute-done.1 = bf16[256,2048]{1,0:T(8,128)(2,1)} collective-permute-done((bf16[256,2048]{1,0:T(8,128)(2,1)}, bf16[256,2048]{1,0:T(8,128)(2,1)}, u32[]{:S(2)}, u32[]{:S(2)}) %collective-permute-start.1) | collective-permute-done | bytes 1048608 | tf_op jit(solution)/shard_map/ppermute | solution.py:23
  29.2 1.3 constant_dynamic-update-slice_fusion
  30.5 0.6 fusion.7
  31.1 0.6 fusion.4
  31.7 0.1 pad_maximum_fusion.app_ref
  31.8 1.6 %shard_map.77.packed_ref = bf16[2048,1152]{1,0:T(8,128)(2,1)S(1)} custom-call(bf16[256,2048]{1,0:T(8,128)(2,1)S(1)} %copy-done.1, bf16[256,2048]{1,0:T(8,128)(2,1)S(1)} %pad_maximum_fusion.app_ref), custom_call_target="tpu_custom_call" | custom-call | tf_op jit(solution)/shard_map/pallas_call | solution.py:324
  33.4 0.0 copy-start
  33.4 2.1 %copy-done = bf16[2048,1152]{1,0:T(8,128)(2,1)} copy-done((bf16[2048,1152]{1,0:T(8,128)(2,1)}, bf16[2048,1152]{1,0:T(8,128)(2,1)S(1)}, u32[]{:S(2)}) %copy-start) | copy-done | bytes 4718616
  35.6 104.1 %shard_map.78 = (bf16[256,2048]{1,0:T(8,128)(2,1)}, f32[256,2048]{1,0:T(8,128)}) custom-call(bf16[2048,1152]{1,0:T(8,128)(2,1)} %copy-done, bf16[256,2048]{1,0:T(8,128)(2,1)} %orb_ref.1, bf16[256,2048]{1,0:T(8,128)(2,1)} %rot_ref.3, bf16[256,640]{1,0:T(8,128)(2,1)} %bitcast.14), custom_call_target="tpu_custom_call" | custom-call | tf_op jit(solution)/shard_map/pallas_call | solution.py:286
  139.6 0.0 copy-start.2
  139.7 2.5 %copy.22 = bf16[256,2048]{1,0:T(8,128)(2,1)} copy(bf16[256,2048]{1,0:T(8,128)(2,1)} %get-tuple-element.10) | data formatting | bytes 2097152
  142.1 0.0 copy-done.2
  142.1 1.3 copy.23
  (2 shorter events, 0.0 us)
Async XLA Ops:
  0.6 15.8 %collective-permute-start = (bf16[256,2048]{1,0:T(8,128)(2,1)}, bf16[256,2048]{1,0:T(8,128)(2,1)}, u32[]{:S(2)}, u32[]{:S(2)}) collective-permute-start(bf16[256,2048]{1,0:T(8,128)(2,1)} %rot_ref.3), channel_id=1, source_target_pairs={{0,1},{1,2},{2,3},{3,4},{4,5},{5,6},{6,7},{7,8},{8,9},{9,10},{10,1... | collective-permute-start | bytes 3145736 | tf_op jit(solution)/shard_map/ppermute | solution.py:22
  4.3 24.8 %collective-permute-start.1 = (bf16[256,2048]{1,0:T(8,128)(2,1)}, bf16[256,2048]{1,0:T(8,128)(2,1)}, u32[]{:S(2)}, u32[]{:S(2)}) collective-permute-start(bf16[256,2048]{1,0:T(8,128)(2,1)} %rot_ref.3), channel_id=1, source_target_pairs={{1,0},{2,1},{3,2},{4,3},{5,4},{6,5},{7,6},{8,7},{9,8},{10,9},{11,1... | collective-permute-start | bytes 3145736 | tf_op jit(solution)/shard_map/ppermute | solution.py:23
  8.2 9.5 %copy-start.1 = (bf16[256,2048]{1,0:T(8,128)(2,1)S(1)}, bf16[256,2048]{1,0:T(8,128)(2,1)}, u32[]{:S(2)}) copy-start(bf16[256,2048]{1,0:T(8,128)(2,1)} %rot_ref.3) | copy-start | bytes 3145732
  33.4 2.1 %copy-start = (bf16[2048,1152]{1,0:T(8,128)(2,1)}, bf16[2048,1152]{1,0:T(8,128)(2,1)S(1)}, u32[]{:S(2)}) copy-start(bf16[2048,1152]{1,0:T(8,128)(2,1)S(1)} %shard_map.77.packed_ref) | copy-start | bytes 14155780
  139.6 2.5 %copy-start.2 = (f32[256,2048]{1,0:T(8,128)S(1)}, f32[256,2048]{1,0:T(8,128)}, u32[]{:S(2)}) copy-start(f32[256,2048]{1,0:T(8,128)} %get-tuple-element.11) | copy-start | bytes 6291460
